TPU v7x, 512 devices: a whole 4x8x8 slice. The times are simulated.
512 devices in a mesh: slide: 8 (over y), seq: 64 (over x, z, core).
Axes of the slice: x: 4, y: 8, z: 8, core: 2. Of those that a mesh axis runs over, the one named last changes fastest.
Arguments:
- tile_embeddings: bfloat16 [131072, 1536], P(('slide', 'seq')), parts along dimension 0, may hold values from -16 to 16
- tile_position: int32 [131072], P(('slide', 'seq')), parts along dimension 0, may hold values from -1 to 8191, as said below
- input_weight: bfloat16 [1536, 768], P('seq'), may hold values from -0.15625 to 0.15625
- attention_weight: bfloat16 [768, 1152], replicated, may hold values from -0.28867513 to 0.28867513
Outputs:
- attended: bfloat16 [65536, 384], P(('slide', 'seq')), parts along dimension 0
There are 8 independent parts, one for each index of `slide`. A program takes and returns all parts, laid end to end along the dimension named above; an argument that names none is the same for every part. Nothing has to cross between parts.
Inputs may be any that keep to these rules, and one draw needn't show every extreme that they name: `tile_position`: every position 0 to 8191 stands in exactly one slot; all other slots hold -1. Among the slots of one device at most 8 hold positions of one owner block (positions with equal p // 128), and every owner block gets exactly 8 from some device.
All inputs are finite; a program needn't handle non-finite values.
Results may differ from a plain program's by a relative error of at most 0.012.
The roundings to bfloat16 on the way count: a program that leaves them out, or rounds other values in their place, can miss the bound.
Values may be sent and summed in bfloat16 or wider, within the bound.
A program may use at most 64 MiB of HBM per device.

v0:
```python
import jax
import jax.numpy as jnp
from jax import lax
from jax.sharding import PartitionSpec as P

HEADS = 6
TOK_DEV = 128
BRANCHES = 3


def for_sending(x):
    return jax.tree.map(lambda a: a.astype(jnp.bfloat16) if a.dtype == jnp.float32 else a, x)


def from_partner(value, axis, apart):
    mask = 2**apart
    pairs = [(source, source ^ mask) for source in range(lax.axis_size(axis))]
    return lax.ppermute(value, axis, pairs)


def merge_state(earlier, latest, covered_mask):
    joint_max = jnp.maximum(earlier[0], latest[0])
    keep_scale = jnp.exp(earlier[0] - joint_max)
    take_scale = jnp.exp(latest[0] - joint_max)
    combined_total = earlier[1] * keep_scale + latest[1] * take_scale
    joint_sum = earlier[2] * keep_scale[..., None] + latest[2] * take_scale[..., None]
    return (
        jnp.where(covered_mask, joint_max, earlier[0]),
        jnp.where(covered_mask, combined_total, earlier[1]),
        jnp.where(covered_mask[..., None], joint_sum, earlier[2]),
    )


def select_rows(source, stride, head_picks):
    row_count = source.shape[0] // stride
    head_count = len(head_picks)
    divided_rows = source.reshape(row_count, stride, head_count, source.shape[1] // head_count)
    onehot_indicator = (jnp.arange(stride)[:, None] == jnp.array(head_picks)[None, :]).astype(
        source.dtype
    )
    selected_tiles = jnp.einsum(
        "pwbt,wb->pbt", divided_rows, onehot_indicator, preferred_element_type=jnp.float32
    )
    return selected_tiles.astype(source.dtype).reshape(row_count, source.shape[1])


def widen_group(key_pair, bit_level):
    partner = jax.tree.map(
        lambda part, own: part.astype(own.dtype),
        from_partner(for_sending(key_pair), "seq", bit_level),
        key_pair,
    )
    is_lower = lax.axis_index("seq") // 2**bit_level % 2 == 0
    return tuple(
        (
            jnp.where(
                is_lower,
                jnp.concatenate([own_part, theirs], 0),
                jnp.concatenate([theirs, own_part], 0),
            )
            for own_part, theirs in zip(key_pair, partner)
        )
    )


def project(row_block, input_weight):
    return jnp.dot(
        row_block,
        lax.all_gather(input_weight, "seq", axis=0, tiled=True),
        preferred_element_type=jnp.float32,
    ).astype(jnp.bfloat16)


def place_rows(row_block, received_positions):
    flat_spots = received_positions.reshape(-1).astype(jnp.int32)
    flat_rows = row_block.reshape(-1, row_block.shape[-1])
    return (
        jnp.zeros((TOK_DEV, flat_rows.shape[1]), flat_rows.dtype)
        .at[flat_spots]
        .set(flat_rows, mode="drop")
    )


def local(tile_embeddings, tile_position, input_weight, attention_weight):
    devices = lax.axis_size("seq")
    all_width = attention_weight.shape[1] // 3
    head_count = HEADS
    head_width = all_width // head_count
    per_neighbor = 4 * TOK_DEV // devices
    is_kept = tile_position >= 0
    owners = jnp.where(is_kept, tile_position // TOK_DEV, devices)
    offset = jnp.where(is_kept, tile_position % TOK_DEV, TOK_DEV)
    onehot_indicator = (owners[:, None] == jnp.arange(devices)[None, :]).astype(jnp.int32)
    ranking = jnp.sum(jnp.cumsum(onehot_indicator, axis=0) * onehot_indicator, axis=1) - 1
    destination_index = jnp.where(is_kept, owners * per_neighbor + ranking, devices * per_neighbor)
    spot_marks = (
        jnp.full((devices * per_neighbor,), TOK_DEV, jnp.int32)
        .at[destination_index]
        .set(offset, mode="drop")
    )
    spot_marks = spot_marks.astype(jnp.bfloat16).reshape(devices, per_neighbor)
    outgoing = (
        jnp.zeros((devices * per_neighbor, tile_embeddings.shape[1]), jnp.bfloat16)
        .at[destination_index]
        .set(tile_embeddings, mode="drop")
    )
    arrived, received_positions = (
        lax.all_to_all(
            outgoing.reshape(devices, per_neighbor, -1),
            "seq",
            split_axis=0,
            concat_axis=0,
            tiled=True,
        ),
        lax.all_to_all(spot_marks, "seq", split_axis=0, concat_axis=0, tiled=True),
    )
    sequence = project(place_rows(arrived, received_positions), input_weight)
    projections = jnp.dot(sequence, attention_weight, preferred_element_type=jnp.float32).astype(
        jnp.bfloat16
    )
    queries = projections[:, :all_width]
    key_rows = projections[:, all_width : 2 * all_width]
    values = projections[:, 2 * all_width :]
    base_bits = (devices // 8).bit_length() - 1
    gathered = []
    for branch in range(BRANCHES):
        stride = 2**branch
        head_picks = [head_index % stride for head_index in range(head_count)]
        key_pair = tuple((select_rows(member, stride, head_picks) for member in (key_rows, values)))
        for bit_level in range(base_bits + branch):
            key_pair = widen_group(key_pair, bit_level)
        gathered.append(key_pair)
    merged = None
    for branch in range(BRANCHES):
        stride = 2**branch
        head_picks = [head_index % stride for head_index in range(head_count)]
        local_rows = select_rows(queries, stride, head_picks).reshape(-1, head_count, head_width)
        near_keys = gathered[branch][0].reshape(-1, head_count, head_width)
        near_values = gathered[branch][1].reshape(-1, head_count, head_width)
        scores = jnp.einsum(
            "qhd,khd->hqk", local_rows, near_keys, preferred_element_type=jnp.float32
        ) * head_width ** (-0.5)
        row_max = jnp.max(scores, axis=2)
        weights = jnp.exp(scores - row_max[..., None])
        row_total = jnp.sum(weights, axis=2)
        weighted = jnp.einsum(
            "hqk,khd->hqd",
            weights.astype(jnp.bfloat16),
            near_values,
            preferred_element_type=jnp.float32,
        )
        if branch == 0:
            merged = (row_max, row_total, weighted)
        else:
            row_count = TOK_DEV // stride
            covered_mask = (jnp.arange(stride)[None, :] == jnp.array(head_picks)[:, None])[
                :, None, :
            ]
            strided = (
                merged[0].reshape(head_count, row_count, stride),
                merged[1].reshape(head_count, row_count, stride),
                merged[2].reshape(head_count, row_count, stride, head_width),
            )
            strided = merge_state(
                strided,
                (row_max[..., None], row_total[..., None], weighted[:, :, None, :]),
                covered_mask,
            )
            merged = (
                strided[0].reshape(head_count, TOK_DEV),
                strided[1].reshape(head_count, TOK_DEV),
                strided[2].reshape(head_count, TOK_DEV, head_width),
            )
    result = merged[2] / merged[1][..., None]
    return jnp.transpose(result, (1, 0, 2)).reshape(TOK_DEV, all_width).astype(jnp.bfloat16)


def solution(mesh):
    in_specs = (P(("slide", "seq"), None), P(("slide", "seq")), P("seq", None), P())
    out_specs = P(("slide", "seq"), None)
    return jax.shard_map(local, mesh=mesh, in_specs=in_specs, out_specs=out_specs, check_vma=False)
```

profile of v0, /device:TPU:1, one launch (start us, length us, event | category | flops | bytes accessed | tf_op | source)
XLA Modules:
  0.0 289.3 jit_solution(17616280735578941183)
XLA Ops:
  10.3 1.4 scatter_custom_fusion
  12.4 14.8 %all-to-all-start = ((bf16[64,1,8]{2,1,0:T(2,128)(2,1)}), bf16[64,1,8]{2,1,0:T(2,128)(2,1)S(1)}, u32[]{:S(2)}, u32[]{:S(2)}) async-start(bf16[64,1,8]{2,1,0:T(2,128)(2,1)} %all_to_all.12), calls=%async_computation | async-start | bytes 65536 | tf_op jit(solution)/shard_map/all_to_all | solution.py:115
  27.3 3.7 %scatter_custom_fusion.1 = bf16[512,1536]{1,0:T(8,128)(2,1)} fusion(s32[256]{0:T(256)S(1)} %get-tuple-element.18, bf16[256,1536]{1,0:T(8,128)(2,1)} %param.15, bf16[]{:T(256)} %constant.154.clone.1), kind=kCustom, calls=%fused_computation.60 | custom fusion | bytes 1573376 | tf_op jit(solution)/shard_map/scatter | solution.py:105
  31.0 5.5 %all-to-all-done = bf16[64,1,8]{2,1,0:T(2,128)(2,1)S(1)} async-done(((bf16[64,1,8]{2,1,0:T(2,128)(2,1)}), bf16[64,1,8]{2,1,0:T(2,128)(2,1)S(1)}, u32[]{:S(2)}, u32[]{:S(2)}) %all-to-all-start) | async-done | bytes 1056 | tf_op jit(solution)/shard_map/all_to_all | solution.py:115
  36.5 5.0 %all-to-all-start.1 = ((bf16[64,8,1536]{2,1,0:T(8,128)(2,1)}), bf16[64,8,1536]{2,1,0:T(8,128)(2,1)S(1)}, u32[]{:S(2)}, u32[]{:S(2)}) async-start(bf16[64,8,1536]{2,1,0:T(8,128)(2,1)} %bitcast.11), calls=%async_computation.1 | async-start | bytes 3145728 | tf_op jit(solution)/shard_map/all_to_all | solution.py:108
  42.6 40.5 %all-to-all-done.1 = bf16[64,8,1536]{2,1,0:T(8,128)(2,1)S(1)} async-done(((bf16[64,8,1536]{2,1,0:T(8,128)(2,1)}), bf16[64,8,1536]{2,1,0:T(8,128)(2,1)S(1)}, u32[]{:S(2)}, u32[]{:S(2)}) %all-to-all-start.1) | async-done | bytes 1572896 | tf_op jit(solution)/shard_map/all_to_all | solution.py:108
  83.1 3.6 %scatter_custom_fusion.2 = bf16[128,1536]{1,0:T(8,128)(2,1)} fusion(s32[512]{0:T(512)S(1)} %bitcast.144, bf16[64,8,1536]{2,1,0:T(8,128)(2,1)S(1)} %all-to-all-done.1, bf16[]{:T(256)} %constant.154.clone.1), kind=kCustom, calls=%fused_computation.9 | custom fusion | bytes 1966082 | tf_op jit(solution)/shard_map/scatter | solution.py:80
  86.6 15.8 %all-gather.2.cloned.1.call-done = bf16[1536,768]{1,0:T(8,128)(2,1)} async-done(((bf16[24,768]{1,0:T(8,128)(2,1)}), bf16[1536,768]{1,0:T(8,128)(2,1)}) %all-gather.2.cloned.1.call-update) | async-done | bytes 2359312 | tf_op jit(solution)/shard_map/all_gather | solution.py:69
  102.4 2.8 convolution_convert_fusion
  106.0 2.1 collective-permute-start.3
  108.9 0.9 reshape.455
  109.8 0.9 reshape.450
  111.0 2.2 collective-permute-start
  114.1 2.2 collective-permute-start.19
  116.3 2.2 collective-permute-start.14
  119.0 2.3 collective-permute-start.6
  121.3 2.0 fusion.60
  123.3 1.8 fusion.58
  125.9 2.2 collective-permute-start.10
  128.2 2.6 collective-permute-start.20
  130.9 2.7 collective-permute-start.15
  133.9 2.6 collective-permute-start.7
  136.8 2.7 collective-permute-start.11
  140.4 3.3 %collective-permute-start.21 = (bf16[128,384]{0,1:T(8,128)(2,1)S(1)}, bf16[128,384]{0,1:T(8,128)(2,1)S(1)}, u32[]{:S(2)}, u32[]{:S(2)}) collective-permute-start(bf16[128,384]{0,1:T(8,128)(2,1)S(1)} %maximum_select_fusion.45), channel_id=1, source_target_pairs={{0,4},{1,5},{2,6},{3,7},{4,0},{5,1},{6,2},{7,3},{8,12},{9,13},{10,... | collective-permute-start | bytes 294920 | tf_op jit(solution)/shard_map/ppermute | solution.py:18
  145.2 2.9 %collective-permute-start.16 = (bf16[128,384]{0,1:T(8,128)(2,1)}, bf16[128,384]{0,1:T(8,128)(2,1)}, u32[]{:S(2)}, u32[]{:S(2)}) collective-permute-start(bf16[128,384]{0,1:T(8,128)(2,1)} %maximum_select_fusion.42), channel_id=1, source_target_pairs={{0,4},{1,5},{2,6},{3,7},{4,0},{5,1},{6,2},{7,3},{8,12},{9,13},{10,... | collective-permute-start | bytes 294920 | tf_op jit(solution)/shard_map/ppermute | solution.py:18
  148.3 2.6 collective-permute-start.1
  151.0 2.0 maximum_select_fusion.24
  153.1 2.7 collective-permute-start.4
  155.9 3.3 %collective-permute-start.12 = (bf16[256,384]{0,1:T(8,128)(2,1)S(1)}, bf16[256,384]{0,1:T(8,128)(2,1)}, u32[]{:S(2)}, u32[]{:S(2)}) collective-permute-start(bf16[256,384]{0,1:T(8,128)(2,1)S(1)} %maximum_select_fusion.31), channel_id=1, source_target_pairs={{0,4},{1,5},{2,6},{3,7},{4,0},{5,1},{6,2},{7,3},{8,12},{9,13},{10,... | collective-permute-start | bytes 589832 | tf_op jit(solution)/shard_map/ppermute | solution.py:18
  159.4 2.9 %collective-permute-start.8 = (bf16[256,384]{0,1:T(8,128)(2,1)S(1)}, bf16[256,384]{0,1:T(8,128)(2,1)}, u32[]{:S(2)}, u32[]{:S(2)}) collective-permute-start(bf16[256,384]{0,1:T(8,128)(2,1)S(1)} %maximum_select_fusion.29), channel_id=1, source_target_pairs={{0,4},{1,5},{2,6},{3,7},{4,0},{5,1},{6,2},{7,3},{8,12},{9,13},{10,... | collective-permute-start | bytes 589832 | tf_op jit(solution)/shard_map/ppermute | solution.py:18
  162.3 1.1 maximum_select_fusion.33
  163.4 4.3 %collective-permute-start.17 = (bf16[256,384]{0,1:T(8,128)(2,1)S(1)}, bf16[256,384]{0,1:T(8,128)(2,1)}, u32[]{:S(2)}, u32[]{:S(2)}) collective-permute-start(bf16[256,384]{0,1:T(8,128)(2,1)S(1)} %maximum_select_fusion.33), channel_id=1, source_target_pairs={{0,8},{1,9},{2,10},{3,11},{4,12},{5,13},{6,14},{7,15},{8,0},{9,1},... | collective-permute-start | bytes 589832 | tf_op jit(solution)/shard_map/ppermute | solution.py:18
  167.7 1.0 maximum_select_fusion.34
  168.8 1.0 maximum_select_fusion.32
  169.8 1.7 maximum_select_fusion.35
  171.5 4.9 %collective-permute-start.22 = (bf16[256,384]{0,1:T(8,128)(2,1)}, bf16[256,384]{0,1:T(8,128)(2,1)}, u32[]{:S(2)}, u32[]{:S(2)}) collective-permute-start(bf16[256,384]{0,1:T(8,128)(2,1)} %maximum_select_fusion.35), channel_id=1, source_target_pairs={{0,8},{1,9},{2,10},{3,11},{4,12},{5,13},{6,14},{7,15},{8,0},{9,1},... | collective-permute-start | bytes 589832 | tf_op jit(solution)/shard_map/ppermute | solution.py:18
  176.5 0.9 maximum_select_fusion.15
  177.3 3.2 %collective-permute-start.5 = (bf16[512,384]{1,0:T(8,128)(2,1)}, bf16[512,384]{1,0:T(8,128)(2,1)}, u32[]{:S(2)}, u32[]{:S(2)}) collective-permute-start(bf16[512,384]{1,0:T(8,128)(2,1)} %maximum_select_fusion.15), channel_id=1, source_target_pairs={{0,4},{1,5},{2,6},{3,7},{4,0},{5,1},{6,2},{7,3},{8,12},{9,13},{10,... | collective-permute-start | bytes 1179656 | tf_op jit(solution)/shard_map/ppermute | solution.py:18
  181.4 2.1 maximum_select_fusion.12
  183.5 1.7 copy.62
  185.2 2.1 maximum_select_fusion.14
  187.4 14.7 %collective-permute-done.8 = bf16[256,384]{0,1:T(8,128)(2,1)} collective-permute-done((bf16[256,384]{0,1:T(8,128)(2,1)S(1)}, bf16[256,384]{0,1:T(8,128)(2,1)}, u32[]{:S(2)}, u32[]{:S(2)}) %collective-permute-start.8) | collective-permute-done | bytes 196640 | tf_op jit(solution)/shard_map/ppermute | solution.py:18
  202.1 1.9 collective-permute-start.2
  204.0 1.9 maximum_select_fusion.17
  205.9 4.0 %collective-permute-start.9 = (bf16[512,384]{0,1:T(8,128)(2,1)}, bf16[512,384]{0,1:T(8,128)(2,1)}, u32[]{:S(2)}, u32[]{:S(2)}) collective-permute-start(bf16[512,384]{0,1:T(8,128)(2,1)} %maximum_select_fusion.17), channel_id=1, source_target_pairs={{0,8},{1,9},{2,10},{3,11},{4,12},{5,13},{6,14},{7,15},{8,0},{9,1},... | collective-permute-start | bytes 1179656 | tf_op jit(solution)/shard_map/ppermute | solution.py:18
  209.9 1.9 maximum_select_fusion.18
  211.8 1.9 maximum_select_fusion.16
  213.7 1.9 maximum_select_fusion.19
  215.5 5.2 %collective-permute-start.13 = (bf16[512,384]{0,1:T(8,128)(2,1)}, bf16[512,384]{0,1:T(8,128)(2,1)}, u32[]{:S(2)}, u32[]{:S(2)}) collective-permute-start(bf16[512,384]{0,1:T(8,128)(2,1)} %maximum_select_fusion.19), channel_id=1, source_target_pairs={{0,8},{1,9},{2,10},{3,11},{4,12},{5,13},{6,14},{7,15},{8,0},{9,1},... | collective-permute-start | bytes 1179656 | tf_op jit(solution)/shard_map/ppermute | solution.py:18
  220.7 2.1 maximum_select_fusion.23
  222.8 3.3 %collective-permute-start.23 = (bf16[512,384]{0,1:T(8,128)(2,1)}, bf16[512,384]{0,1:T(8,128)(2,1)}, u32[]{:S(2)}, u32[]{:S(2)}) collective-permute-start(bf16[512,384]{0,1:T(8,128)(2,1)} %maximum_select_fusion.23), channel_id=1, source_target_pairs={{0,16},{1,17},{2,18},{3,19},{4,20},{5,21},{6,22},{7,23},{8,24},{9,... | collective-permute-start | bytes 1179656 | tf_op jit(solution)/shard_map/ppermute | solution.py:18
  226.1 1.9 maximum_select_fusion.20
  228.0 1.9 maximum_select_fusion.22
  229.8 1.9 maximum_select_fusion.21
  231.7 29.4 %collective-permute-done.2 = bf16[512,384]{1,0:T(8,128)(2,1)} collective-permute-done((bf16[512,384]{1,0:T(8,128)(2,1)S(1)}, bf16[512,384]{1,0:T(8,128)(2,1)}, u32[]{:S(2)}, u32[]{:S(2)}) %collective-permute-start.2) | collective-permute-done | bytes 393248 | tf_op jit(solution)/shard_map/ppermute | solution.py:18
  261.1 3.3 %collective-permute-start.18 = (bf16[512,384]{0,1:T(8,128)(2,1)}, bf16[512,384]{0,1:T(8,128)(2,1)}, u32[]{:S(2)}, u32[]{:S(2)}) collective-permute-start(bf16[512,384]{0,1:T(8,128)(2,1)} %maximum_select_fusion.21), channel_id=1, source_target_pairs={{0,16},{1,17},{2,18},{3,19},{4,20},{5,21},{6,22},{7,23},{8,24},{9,... | collective-permute-start | bytes 1179656 | tf_op jit(solution)/shard_map/ppermute | solution.py:18
  264.4 1.2 copy.59
  267.0 0.9 copy-done.1
  267.9 1.2 copy.63
  269.1 3.5 %fusion.2 = f32[6,128,64]{1,2,0:T(8,128)} fusion(f32[6,128,1024]{2,1,0:T(8,128)} %copy-done.1, f32[6,128]{1,0:T(8,128)S(1)} %get-tuple-element.25, bf16[512,6,64]{0,2,1:T(8,128)(2,1)S(1)} %bitcast.124, bf16[512,6,64]{0,2,1:T(8,128)(2,1)S(1)} %copy-done.4, pred[]{:T(512)S(6)} %eq.206), kind=kOutput, calls=%fused_computation.8 | convolution fusion | flops 106561536 | bytes 4131841 | tf_op jit(solution)/shard_map/hqk,khd->hqd/dot_general | solution.py:146
  272.6 1.6 fusion.94
  275.0 1.9 fusion.10
  277.3 1.8 fusion.93
  279.8 1.6 fusion.38
  (138 shorter events, 18.4 us)
Async XLA Ops:
  6.5 95.9 %copy-start = (bf16[768,1152]{1,0:T(8,128)(2,1)S(1)}, bf16[768,1152]{1,0:T(8,128)(2,1)}, u32[]{:S(2)}) copy-start(bf16[768,1152]{1,0:T(8,128)(2,1)} %param.18) | copy-start | bytes 5308420
  6.5 95.9 %all-gather.2.cloned.1.call-start = ((), (), s32[]{:S(2)}) async-start(), calls=%async_computation.2 | async-start | bytes 2396160 | tf_op jit(solution)/shard_map/all_gather | solution.py:69
  12.4 24.1 %all-to-all-start = ((bf16[64,1,8]{2,1,0:T(2,128)(2,1)}), bf16[64,1,8]{2,1,0:T(2,128)(2,1)S(1)}, u32[]{:S(2)}, u32[]{:S(2)}) async-start(bf16[64,1,8]{2,1,0:T(2,128)(2,1)} %all_to_all.12), calls=%async_computation | async-start | bytes 65536 | tf_op jit(solution)/shard_map/all_to_all | solution.py:115
  36.5 5.1 %copy-start.14 = (s32[6]{0:T(128)S(1)}, s32[6]{0:T(128)}, u32[]{:S(2)}) copy-start(s32[6]{0:T(128)} %constant.172.clone) | copy-start | bytes 76
  36.5 5.2 %copy-start.15 = (s32[6]{0:T(128)S(1)}, s32[6]{0:T(128)}, u32[]{:S(2)}) copy-start(s32[6]{0:T(128)} %constant.173.clone) | copy-start | bytes 76
  36.5 46.6 %all-to-all-start.1 = ((bf16[64,8,1536]{2,1,0:T(8,128)(2,1)}), bf16[64,8,1536]{2,1,0:T(8,128)(2,1)S(1)}, u32[]{:S(2)}, u32[]{:S(2)}) async-start(bf16[64,8,1536]{2,1,0:T(8,128)(2,1)} %bitcast.11), calls=%async_computation.1 | async-start | bytes 3145728 | tf_op jit(solution)/shard_map/all_to_all | solution.py:108
  106.0 42.3 %collective-permute-start.3 = (bf16[128,384]{1,0:T(8,128)(2,1)S(1)}, bf16[128,384]{1,0:T(8,128)(2,1)S(1)}, u32[]{:S(2)}, u32[]{:S(2)}) collective-permute-start(bf16[128,384]{1,0:T(8,128)(2,1)S(1)} %get-tuple-element.15), channel_id=1, source_target_pairs={{0,1},{1,0},{2,3},{3,2},{4,5},{5,4},{6,7},{7,6},{8,9},{9,8},{10,11... | collective-permute-start | bytes 294920 | tf_op jit(solution)/shard_map/ppermute | solution.py:18
  111.0 34.2 %collective-permute-start = (bf16[128,384]{1,0:T(8,128)(2,1)S(1)}, bf16[128,384]{1,0:T(8,128)(2,1)S(1)}, u32[]{:S(2)}, u32[]{:S(2)}) collective-permute-start(bf16[128,384]{1,0:T(8,128)(2,1)S(1)} %get-tuple-element.16), channel_id=1, source_target_pairs={{0,1},{1,0},{2,3},{3,2},{4,5},{5,4},{6,7},{7,6},{8,9},{9,8},{10,11... | collective-permute-start | bytes 294920 | tf_op jit(solution)/shard_map/ppermute | solution.py:18
  114.1 11.8 %collective-permute-start.19 = (bf16[32,384]{0,1:T(8,128)(2,1)S(1)}, bf16[32,384]{0,1:T(8,128)(2,1)S(1)}, u32[]{:S(2)}, u32[]{:S(2)}) collective-permute-start(bf16[32,384]{0,1:T(8,128)(2,1)S(1)} %bitcast.127), channel_id=1, source_target_pairs={{0,1},{1,0},{2,3},{3,2},{4,5},{5,4},{6,7},{7,6},{8,9},{9,8},{10,11... | collective-permute-start | bytes 73736 | tf_op jit(solution)/shard_map/ppermute | solution.py:18
  116.3 11.9 %collective-permute-start.14 = (bf16[32,384]{0,1:T(8,128)(2,1)S(1)}, bf16[32,384]{0,1:T(8,128)(2,1)S(1)}, u32[]{:S(2)}, u32[]{:S(2)}) collective-permute-start(bf16[32,384]{0,1:T(8,128)(2,1)S(1)} %bitcast.125), channel_id=1, source_target_pairs={{0,1},{1,0},{2,3},{3,2},{4,5},{5,4},{6,7},{7,6},{8,9},{9,8},{10,11... | collective-permute-start | bytes 73736 | tf_op jit(solution)/shard_map/ppermute | solution.py:18
  119.0 11.9 %collective-permute-start.6 = (bf16[64,384]{0,1:T(8,128)(2,1)S(1)}, bf16[64,384]{0,1:T(8,128)(2,1)S(1)}, u32[]{:S(2)}, u32[]{:S(2)}) collective-permute-start(bf16[64,384]{0,1:T(8,128)(2,1)S(1)} %bitcast.116), channel_id=1, source_target_pairs={{0,1},{1,0},{2,3},{3,2},{4,5},{5,4},{6,7},{7,6},{8,9},{9,8},{10,11... | collective-permute-start | bytes 147464 | tf_op jit(solution)/shard_map/ppermute | solution.py:18
  125.9 8.0 %collective-permute-start.10 = (bf16[64,384]{0,1:T(8,128)(2,1)S(1)}, bf16[64,384]{0,1:T(8,128)(2,1)S(1)}, u32[]{:S(2)}, u32[]{:S(2)}) collective-permute-start(bf16[64,384]{0,1:T(8,128)(2,1)S(1)} %bitcast.113), channel_id=1, source_target_pairs={{0,1},{1,0},{2,3},{3,2},{4,5},{5,4},{6,7},{7,6},{8,9},{9,8},{10,11... | collective-permute-start | bytes 147464 | tf_op jit(solution)/shard_map/ppermute | solution.py:18
  128.2 8.6 %collective-permute-start.20 = (bf16[64,384]{0,1:T(8,128)(2,1)S(1)}, bf16[64,384]{0,1:T(8,128)(2,1)S(1)}, u32[]{:S(2)}, u32[]{:S(2)}) collective-permute-start(bf16[64,384]{0,1:T(8,128)(2,1)S(1)} %maximum_select_fusion.43), channel_id=1, source_target_pairs={{0,2},{1,3},{2,0},{3,1},{4,6},{5,7},{6,4},{7,5},{8,10},{9,11},{10,... | collective-permute-start | bytes 147464 | tf_op jit(solution)/shard_map/ppermute | solution.py:18
  130.9 9.5 %collective-permute-start.15 = (bf16[64,384]{0,1:T(8,128)(2,1)S(1)}, bf16[64,384]{0,1:T(8,128)(2,1)S(1)}, u32[]{:S(2)}, u32[]{:S(2)}) collective-permute-start(bf16[64,384]{0,1:T(8,128)(2,1)S(1)} %maximum_select_fusion.40), channel_id=1, source_target_pairs={{0,2},{1,3},{2,0},{3,1},{4,6},{5,7},{6,4},{7,5},{8,10},{9,11},{10,... | collective-permute-start | bytes 147464 | tf_op jit(solution)/shard_map/ppermute | solution.py:18
  133.9 21.9 %collective-permute-start.7 = (bf16[128,384]{0,1:T(8,128)(2,1)S(1)}, bf16[128,384]{0,1:T(8,128)(2,1)S(1)}, u32[]{:S(2)}, u32[]{:S(2)}) collective-permute-start(bf16[128,384]{0,1:T(8,128)(2,1)S(1)} %maximum_select_fusion.37), channel_id=1, source_target_pairs={{0,2},{1,3},{2,0},{3,1},{4,6},{5,7},{6,4},{7,5},{8,10},{9,11},{10,... | collective-permute-start | bytes 294920 | tf_op jit(solution)/shard_map/ppermute | solution.py:18
  136.8 16.3 %collective-permute-start.11 = (bf16[128,384]{0,1:T(8,128)(2,1)S(1)}, bf16[128,384]{0,1:T(8,128)(2,1)S(1)}, u32[]{:S(2)}, u32[]{:S(2)}) collective-permute-start(bf16[128,384]{0,1:T(8,128)(2,1)S(1)} %maximum_select_fusion.39), channel_id=1, source_target_pairs={{0,2},{1,3},{2,0},{3,1},{4,6},{5,7},{6,4},{7,5},{8,10},{9,11},{10,... | collective-permute-start | bytes 294920 | tf_op jit(solution)/shard_map/ppermute | solution.py:18
  140.4 18.8 %copy-start.7 = (bf16[128,384]{0,1:T(8,128)(2,1)}, bf16[128,384]{0,1:T(8,128)(2,1)S(1)}, u32[]{:S(2)}) copy-start(bf16[128,384]{0,1:T(8,128)(2,1)S(1)} %maximum_select_fusion.45) | copy-start | bytes 294916
  140.4 23.0 %collective-permute-start.21 = (bf16[128,384]{0,1:T(8,128)(2,1)S(1)}, bf16[128,384]{0,1:T(8,128)(2,1)S(1)}, u32[]{:S(2)}, u32[]{:S(2)}) collective-permute-start(bf16[128,384]{0,1:T(8,128)(2,1)S(1)} %maximum_select_fusion.45), channel_id=1, source_target_pairs={{0,4},{1,5},{2,6},{3,7},{4,0},{5,1},{6,2},{7,3},{8,12},{9,13},{10,... | collective-permute-start | bytes 294920 | tf_op jit(solution)/shard_map/ppermute | solution.py:18
  145.2 14.1 %collective-permute-start.16 = (bf16[128,384]{0,1:T(8,128)(2,1)}, bf16[128,384]{0,1:T(8,128)(2,1)}, u32[]{:S(2)}, u32[]{:S(2)}) collective-permute-start(bf16[128,384]{0,1:T(8,128)(2,1)} %maximum_select_fusion.42), channel_id=1, source_target_pairs={{0,4},{1,5},{2,6},{3,7},{4,0},{5,1},{6,2},{7,3},{8,12},{9,13},{10,... | collective-permute-start | bytes 294920 | tf_op jit(solution)/shard_map/ppermute | solution.py:18
  148.3 29.0 %collective-permute-start.1 = (bf16[256,384]{1,0:T(8,128)(2,1)S(1)}, bf16[256,384]{1,0:T(8,128)(2,1)S(1)}, u32[]{:S(2)}, u32[]{:S(2)}) collective-permute-start(bf16[256,384]{1,0:T(8,128)(2,1)S(1)} %maximum_select_fusion.25), channel_id=1, source_target_pairs={{0,2},{1,3},{2,0},{3,1},{4,6},{5,7},{6,4},{7,5},{8,10},{9,11},{10,... | collective-permute-start | bytes 589832 | tf_op jit(solution)/shard_map/ppermute | solution.py:18
  151.0 16.7 %copy-start.9 = (bf16[128,6,64]{0,2,1:T(8,128)(2,1)S(1)}, bf16[128,6,64]{0,2,1:T(8,128)(2,1)}, u32[]{:S(2)}) copy-start(bf16[128,6,64]{0,2,1:T(8,128)(2,1)} %maximum_select_fusion.44) | copy-start | bytes 294916
  153.0 15.8 %copy-start.11 = (bf16[128,6,64]{0,2,1:T(8,128)(2,1)S(1)}, bf16[128,6,64]{0,2,1:T(8,128)(2,1)}, u32[]{:S(2)}) copy-start(bf16[128,6,64]{0,2,1:T(8,128)(2,1)} %maximum_select_fusion.41) | copy-start | bytes 294916
  153.1 18.5 %collective-permute-start.4 = (bf16[256,384]{1,0:T(8,128)(2,1)S(1)}, bf16[256,384]{1,0:T(8,128)(2,1)S(1)}, u32[]{:S(2)}, u32[]{:S(2)}) collective-permute-start(bf16[256,384]{1,0:T(8,128)(2,1)S(1)} %maximum_select_fusion.27), channel_id=1, source_target_pairs={{0,2},{1,3},{2,0},{3,1},{4,6},{5,7},{6,4},{7,5},{8,10},{9,11},{10,... | collective-permute-start | bytes 589832 | tf_op jit(solution)/shard_map/ppermute | solution.py:18
  155.9 50.0 %collective-permute-start.12 = (bf16[256,384]{0,1:T(8,128)(2,1)S(1)}, bf16[256,384]{0,1:T(8,128)(2,1)}, u32[]{:S(2)}, u32[]{:S(2)}) collective-permute-start(bf16[256,384]{0,1:T(8,128)(2,1)S(1)} %maximum_select_fusion.31), channel_id=1, source_target_pairs={{0,4},{1,5},{2,6},{3,7},{4,0},{5,1},{6,2},{7,3},{8,12},{9,13},{10,... | collective-permute-start | bytes 589832 | tf_op jit(solution)/shard_map/ppermute | solution.py:18
  159.2 10.6 %copy-start.8 = (bf16[128,384]{0,1:T(8,128)(2,1)S(1)}, bf16[128,384]{0,1:T(8,128)(2,1)}, u32[]{:S(2)}) copy-start(bf16[128,384]{0,1:T(8,128)(2,1)} %copy-done.7) | copy-start | bytes 294916
  159.4 42.8 %collective-permute-start.8 = (bf16[256,384]{0,1:T(8,128)(2,1)S(1)}, bf16[256,384]{0,1:T(8,128)(2,1)}, u32[]{:S(2)}, u32[]{:S(2)}) collective-permute-start(bf16[256,384]{0,1:T(8,128)(2,1)S(1)} %maximum_select_fusion.29), channel_id=1, source_target_pairs={{0,4},{1,5},{2,6},{3,7},{4,0},{5,1},{6,2},{7,3},{8,12},{9,13},{10,... | collective-permute-start | bytes 589832 | tf_op jit(solution)/shard_map/ppermute | solution.py:18
  163.4 4.3 %copy-start.10 = (bf16[128,384]{0,1:T(8,128)(2,1)}, bf16[128,384]{0,1:T(8,128)(2,1)S(1)}, u32[]{:S(2)}) copy-start(bf16[128,384]{0,1:T(8,128)(2,1)S(1)} %collective-permute-done.21) | copy-start | bytes 294916
  163.4 59.4 %collective-permute-start.17 = (bf16[256,384]{0,1:T(8,128)(2,1)S(1)}, bf16[256,384]{0,1:T(8,128)(2,1)}, u32[]{:S(2)}, u32[]{:S(2)}) collective-permute-start(bf16[256,384]{0,1:T(8,128)(2,1)S(1)} %maximum_select_fusion.33), channel_id=1, source_target_pairs={{0,8},{1,9},{2,10},{3,11},{4,12},{5,13},{6,14},{7,15},{8,0},{9,1},... | collective-permute-start | bytes 589832 | tf_op jit(solution)/shard_map/ppermute | solution.py:18
  171.5 5.8 %copy-start.2 = (bf16[256,384]{1,0:T(8,128)(2,1)}, bf16[256,384]{1,0:T(8,128)(2,1)S(1)}, u32[]{:S(2)}) copy-start(bf16[256,384]{1,0:T(8,128)(2,1)S(1)} %collective-permute-done.4) | copy-start | bytes 589828
  171.5 44.0 %collective-permute-start.22 = (bf16[256,384]{0,1:T(8,128)(2,1)}, bf16[256,384]{0,1:T(8,128)(2,1)}, u32[]{:S(2)}, u32[]{:S(2)}) collective-permute-start(bf16[256,384]{0,1:T(8,128)(2,1)} %maximum_select_fusion.35), channel_id=1, source_target_pairs={{0,8},{1,9},{2,10},{3,11},{4,12},{5,13},{6,14},{7,15},{8,0},{9,1},... | collective-permute-start | bytes 589832 | tf_op jit(solution)/shard_map/ppermute | solution.py:18
  177.3 90.6 %collective-permute-start.5 = (bf16[512,384]{1,0:T(8,128)(2,1)}, bf16[512,384]{1,0:T(8,128)(2,1)}, u32[]{:S(2)}, u32[]{:S(2)}) collective-permute-start(bf16[512,384]{1,0:T(8,128)(2,1)} %maximum_select_fusion.15), channel_id=1, source_target_pairs={{0,4},{1,5},{2,6},{3,7},{4,0},{5,1},{6,2},{7,3},{8,12},{9,13},{10,... | collective-permute-start | bytes 1179656 | tf_op jit(solution)/shard_map/ppermute | solution.py:18
  202.1 59.0 %collective-permute-start.2 = (bf16[512,384]{1,0:T(8,128)(2,1)S(1)}, bf16[512,384]{1,0:T(8,128)(2,1)}, u32[]{:S(2)}, u32[]{:S(2)}) collective-permute-start(bf16[512,384]{1,0:T(8,128)(2,1)S(1)} %maximum_select_fusion.13), channel_id=1, source_target_pairs={{0,4},{1,5},{2,6},{3,7},{4,0},{5,1},{6,2},{7,3},{8,12},{9,13},{10,... | collective-permute-start | bytes 1179656 | tf_op jit(solution)/shard_map/ppermute | solution.py:18
  205.9 66.7 %collective-permute-start.9 = (bf16[512,384]{0,1:T(8,128)(2,1)}, bf16[512,384]{0,1:T(8,128)(2,1)}, u32[]{:S(2)}, u32[]{:S(2)}) collective-permute-start(bf16[512,384]{0,1:T(8,128)(2,1)} %maximum_select_fusion.17), channel_id=1, source_target_pairs={{0,8},{1,9},{2,10},{3,11},{4,12},{5,13},{6,14},{7,15},{8,0},{9,1},... | collective-permute-start | bytes 1179656 | tf_op jit(solution)/shard_map/ppermute | solution.py:18
  215.5 59.4 %collective-permute-start.13 = (bf16[512,384]{0,1:T(8,128)(2,1)}, bf16[512,384]{0,1:T(8,128)(2,1)}, u32[]{:S(2)}, u32[]{:S(2)}) collective-permute-start(bf16[512,384]{0,1:T(8,128)(2,1)} %maximum_select_fusion.19), channel_id=1, source_target_pairs={{0,8},{1,9},{2,10},{3,11},{4,12},{5,13},{6,14},{7,15},{8,0},{9,1},... | collective-permute-start | bytes 1179656 | tf_op jit(solution)/shard_map/ppermute | solution.py:18
  222.8 57.0 %collective-permute-start.23 = (bf16[512,384]{0,1:T(8,128)(2,1)}, bf16[512,384]{0,1:T(8,128)(2,1)}, u32[]{:S(2)}, u32[]{:S(2)}) collective-permute-start(bf16[512,384]{0,1:T(8,128)(2,1)} %maximum_select_fusion.23), channel_id=1, source_target_pairs={{0,16},{1,17},{2,18},{3,19},{4,20},{5,21},{6,22},{7,23},{8,24},{9,... | collective-permute-start | bytes 1179656 | tf_op jit(solution)/shard_map/ppermute | solution.py:18
  226.1 39.5 %copy-start.5 = (bf16[512,6,64]{0,2,1:T(8,128)(2,1)S(1)}, bf16[512,6,64]{0,2,1:T(8,128)(2,1)}, u32[]{:S(2)}) copy-start(bf16[512,6,64]{0,2,1:T(8,128)(2,1)} %maximum_select_fusion.12) | copy-start | bytes 1179652
  226.1 39.5 %copy-start.13 = (bf16[128,384]{0,1:T(8,128)(2,1)S(1)}, bf16[128,384]{0,1:T(8,128)(2,1)}, u32[]{:S(2)}) copy-start(bf16[128,384]{0,1:T(8,128)(2,1)} %copy.55) | copy-start | bytes 294916
  261.1 16.1 %collective-permute-start.18 = (bf16[512,384]{0,1:T(8,128)(2,1)}, bf16[512,384]{0,1:T(8,128)(2,1)}, u32[]{:S(2)}, u32[]{:S(2)}) collective-permute-start(bf16[512,384]{0,1:T(8,128)(2,1)} %maximum_select_fusion.21), channel_id=1, source_target_pairs={{0,16},{1,17},{2,18},{3,19},{4,20},{5,21},{6,22},{7,23},{8,24},{9,... | collective-permute-start | bytes 1179656 | tf_op jit(solution)/shard_map/ppermute | solution.py:18
  266.3 1.6 copy-start.1
  266.3 2.8 copy-start.4
  269.1 3.5 %copy-start.6 = (bf16[512,6,64]{0,2,1:T(8,128)(2,1)S(1)}, bf16[512,6,64]{0,2,1:T(8,128)(2,1)}, u32[]{:S(2)}) copy-start(bf16[512,6,64]{0,2,1:T(8,128)(2,1)} %maximum_select_fusion.16) | copy-start | bytes 1179652
  269.1 3.5 %copy-start.16 = (f32[6,1,64,64]{3,1,2,0:T(1,128)S(1)}, f32[6,1,64,64]{3,1,2,0:T(1,128)}, u32[]{:S(2)}) copy-start(f32[6,1,64,64]{3,1,2,0:T(1,128)} %fusion.60) | copy-start | bytes 294916
  275.0 2.3 copy-start.17
  277.3 2.5 copy-start.3
  279.8 1.9 copy-start.12
Sparse Core Ops, SparseCore 0:
  10.6 91.7 all-gather.1
where the time goes:
time: 292 us; the launch traced here: 289 us
  waiting for transfers between devices  107 us (37%)
  starting transfers between devices  91.2 us (31%)
  other arithmetic  35.8 us (12%)
  local copies, waits for them, and re-layouts  23.7 us (8%)
  matrix products  17.7 us (6%)
  between operations  14.3 us (5%)
    ppermute x24, starting transfers between devices, from_partner(): return lax.ppermute(value, axis, pairs)  71.4 us
    ppermute x24, waiting for transfers between devices, from_partner(): return lax.ppermute(value, axis, pairs)  44.1 us
    all_to_all x1, waiting for transfers between devices, local(): lax.all_to_all(outgoing.reshape(devices, per_neighbor, -1), 'seq', split_...  40.5 us
    select_n x33, other arithmetic, widen_group(): jnp.where(is_lower, jnp.concatenate([own_part, theirs], 0), jnp.concatena...  30.8 us
    all_gather x1, waiting for transfers between devices, project(): lax.all_gather(input_weight, 'seq', axis=0, tiled=True)  15.8 us
    all_to_all x1, starting transfers between devices, local(): lax.all_to_all(spot_marks, 'seq', split_axis=0, concat_axis=0, tiled=True)  14.8 us
    dot_general x3, matrix products, local(): jnp.einsum('hqk,khd->hqd', weights.astype(jnp.bfloat16), near_values, pre...  7.03 us
  transfers between devices with their start and end apart: 27, of which 5 were waited for; matrix products, arithmetic and copies ran while one was open for 24% of the time, Pallas kernels for 0%

commit v1 on v0

v1 whole, which is shorter than its diff:
```python
import math

import jax
import jax.numpy as jnp
from jax import lax
from jax.experimental import pallas as pl
from jax.experimental.pallas import tpu as pltpu
from jax.sharding import PartitionSpec as P

E = 1536
D = 768
HALF = 384
TOK_DEV = 128
SLOTS = 256
NX = 4
NZ = 8
W_ROWS = 24
EXP2_SCALE = math.log2(math.e) * 64.0 ** -0.5
MESH = pl.DeviceIdType.MESH
F32 = jnp.float32
BF16 = jnp.bfloat16


def iota(shape, dim):
    return lax.broadcasted_iota(jnp.int32, shape, dim)


def nt_dot(a, b):
    return lax.dot_general(a, b, (((1,), (1,)), ((), ())), preferred_element_type=F32)


def roll64(a):
    return jnp.concatenate([a[:, 64:], a[:, :64]], axis=1)


N_COPIES = 160


def kernel(
    emb_ref, pos_ref, w_ref, aw_ref, out_ref,
    emb_own, emb_sib, pos_sib, w_sib, wbuf, awbuf, awc,
    marks, marks_mid, marks_z, marks_got,
    seq, mid, got, xout, kv, c2, qm, m_s, l_s, acc_s, mask_s, fin, seqh,
    send_sems, recv_sems, local_sems,
):
    me = lax.axis_index("seq")
    slide = lax.axis_index("slide")
    x, z, c = me // 16, (me % 16) // 2, me % 2

    def dev(xx, zz, cc):
        return (slide, xx * 16 + zz * 2 + cc)

    sibling = dev(x, z, 1 - c)
    x_of = [(x + d) % NX for d in range(NX)]
    z_of = [(z + d) % NZ for d in range(NZ)]
    right, left = dev(x, z_of[1], c), dev(x, z_of[7], c)
    x_pair = dev(x + 1 - 2 * (x % 2), z, c)

    started = []

    def remote(src, dst, target):
        k = len(started)
        copy = pltpu.make_async_remote_copy(
            src_ref=src, dst_ref=dst, send_sem=send_sems.at[k], recv_sem=recv_sems.at[k],
            device_id=target, device_id_type=MESH,
        )
        started.append(copy)
        copy.start()
        return copy

    emb_load = pltpu.make_async_copy(emb_ref, emb_own, local_sems.at[0])
    emb_load.start()
    aw_load = pltpu.make_async_copy(aw_ref, awbuf, local_sems.at[1])
    aw_load.start()

    barrier = pltpu.get_barrier_semaphore()
    partners = [sibling] + [dev(x_of[d], z, c) for d in (1, 2, 3)] + [dev(x, z_of[d], c) for d in range(1, 8)]
    for partner in partners:
        pl.semaphore_signal(barrier, inc=1, device_id=partner, device_id_type=MESH)
    pl.semaphore_wait(barrier, len(partners))

    w_copy = remote(w_ref.at[:, pl.ds(pl.multiple_of((1 - c) * HALF, 128), HALF)], w_sib, sibling)
    pos_copy = remote(pos_ref, pos_sib, sibling)
    emb_load.wait()
    emb_copy = remote(emb_own, emb_sib, sibling)

    w_copy.wait_recv()
    w_mine = w_ref[:, pl.ds(pl.multiple_of(c * HALF, 128), HALF)].astype(F32)
    w_theirs = w_sib[...].astype(F32)
    first = jnp.where(c == 0, w_mine, w_theirs)
    second = jnp.where(c == 0, w_theirs, w_mine)
    wbuf[x, z] = jnp.concatenate([first, second], axis=0).astype(BF16)

    w_x = {}
    w_right, w_left = {}, {}
    own_block = wbuf.at[x, z]
    for d in (1, 3, 2):
        w_x[d] = remote(own_block, own_block, dev(x_of[d], z, c))
    w_right[0, 0] = remote(own_block, own_block, right)
    w_left[0, 0] = remote(own_block, own_block, left)

    pos_copy.wait_recv()
    pos = jnp.concatenate([pos_ref[...], pos_sib[...]], axis=1)
    slots = 2 * SLOTS
    lane_t = iota((1, slots), 1)
    owner = pos >> 7
    chip = pos >> 8
    owner_hot = iota((64, slots), 0) == owner
    upper = (iota((slots, slots), 0) < iota((slots, slots), 1)) & (
        (iota((slots, slots), 0) // SLOTS) == (iota((slots, slots), 1) // SLOTS)
    )
    before = jnp.dot(
        owner_hot.astype(F32).astype(BF16), upper.astype(F32).astype(BF16), preferred_element_type=F32
    )
    rank = jnp.sum(jnp.where(owner_hot, before, 0.0), axis=0, keepdims=True)
    source_core = jnp.where(lane_t < SLOTS, c, 1 - c)
    target_row = jnp.where(pos >= 0, (owner * 16 + source_core * 8).astype(F32) + rank, -1.0)
    in_chip = jnp.where(pos >= 0, ((owner % 2) * 16 + source_core * 8).astype(F32) + rank, -1.0)
    chip_hot = (iota((32, slots), 0) == chip).astype(F32).astype(BF16)
    value = ((pos & 255) + 1).astype(F32)
    row_kind = (iota((128, slots), 0) % 32).astype(F32)
    marked = jnp.where(row_kind == in_chip, value, 0.0).astype(BF16)
    marks[...] = nt_dot(chip_hot, marked).reshape(NX, 8, 128)

    mark_x = {}
    for d in (1, 3, 2):
        mark_x[d] = remote(marks.at[x_of[d]], marks_mid.at[x], dev(x_of[d], z, c))

    for d in (1, 3, 2):
        w_x[d].wait_recv()
        xo = (x - d) % NX
        block = wbuf.at[xo, z]
        w_right[0, d] = remote(block, block, right)
        w_left[0, d] = remote(block, block, left)

    for d in (1, 3, 2):
        mark_x[d].wait_recv()
    lane_group = iota((8, 128), 1) // 32
    merged = jnp.where(lane_group == x, marks[x], 0.0)
    for d in (1, 3, 2):
        xo = (x - d) % NX
        merged = merged + jnp.where(lane_group == xo, marks_mid[xo], 0.0)
    for zz in range(NZ):
        marks_z[zz] = jnp.broadcast_to(merged[zz : zz + 1], (8, 128))
    mark_z = {}
    for d in range(1, NZ):
        mark_z[d] = remote(marks_z.at[z_of[d]], marks_got.at[z], dev(x, z_of[d], c))

    aw_load.wait()
    lane = iota((D, 128), 1)

    def pair(group_a, group_b):
        a = awbuf[:, group_a * 128 : group_a * 128 + 128].astype(F32)
        b = awbuf[:, group_b * 128 : group_b * 128 + 128].astype(F32)
        even = jnp.where(lane < 64, a, roll64(b))
        odd = jnp.where(lane < 64, roll64(a), b)
        return jnp.where(c == 0, even, odd).astype(BF16)

    awc[:, 0:128] = pair(0, 2)
    awc[:, 128:256] = pair(1, 1)
    awc[:, 256:384] = pair(3, 5)
    awc[:, 384:512] = pair(6, 8)
    awc[:, 512:640] = pair(4, 7)

    for s in (1, 2, 3):
        for d in (0, 1, 3, 2):
            xo = (x - d) % NX
            w_right[s - 1, d].wait_recv()
            block = wbuf.at[xo, (z - s) % NZ]
            w_right[s, d] = remote(block, block, right)
            if s <= 2:
                w_left[s - 1, d].wait_recv()
                block = wbuf.at[xo, (z + s) % NZ]
                w_left[s, d] = remote(block, block, left)
    for d in (0, 1, 3, 2):
        w_left[2, d].wait_recv()
        w_right[3, d].wait_recv()

    weight = wbuf[...].reshape(E, HALF)
    seq[0:SLOTS] = jnp.dot(emb_own[...], weight, preferred_element_type=F32).astype(BF16)
    emb_copy.wait_recv()
    seq[SLOTS:] = jnp.dot(emb_sib[...], weight, preferred_element_type=F32).astype(BF16)

    out_x = {}
    z_sent = {}

    def rows_for(xo):
        hot = (iota((256, slots), 0) + xo * 256).astype(F32) == target_row
        rows = jnp.dot(hot.astype(F32).astype(BF16), seq[...], preferred_element_type=F32)
        return rows.astype(BF16).reshape(NZ, 32, HALF)

    mid[x] = rows_for(x)
    for d in (4, 3, 5, 2, 6, 1, 7):
        z_sent[0, d] = remote(mid.at[x, z_of[d]], got.at[z, x], dev(x, z_of[d], c))
    for d in (2, 1, 3):
        xout[d - 1] = rows_for(x_of[d])
        out_x[d] = remote(xout.at[d - 1], mid.at[x], dev(x_of[d], z, c))
    for d in (1, 3, 2):
        out_x[d].wait_recv()
        xo = (x - d) % NX
        for e in (4, 3, 5, 2, 6, 1, 7):
            z_sent[d, e] = remote(mid.at[xo, z_of[e]], got.at[z, xo], dev(x, z_of[e], c))

    row = iota((256, 128), 0)
    group = row // 64
    wanted = (((row % 64) // 32) * 128 + (row % 32) * 4 + (group % 2) * 2 + group // 2 + 1).astype(F32)

    def place(zo_marks, rows):
        hot = (zo_marks == wanted).astype(F32).astype(BF16)
        return jnp.dot(hot, rows.reshape(128, HALF), preferred_element_type=F32)

    total = place(marks_z[z][0:1], mid[:, z])
    for d in (1, 7, 2, 6, 3, 5, 4):
        mark_z[d].wait_recv()
        for e in range(NX):
            z_sent[e, d].wait_recv()
        zo = (z - d) % NZ
        total = total + place(marks_got[zo][0:1], got[zo])
    seqh[c] = total.astype(BF16)
    half_copy = remote(seqh.at[c], seqh.at[c], sibling)

    def project(h):
        w = awc[pl.ds(pl.multiple_of(h * HALF, 128), HALF), :]
        return jnp.concatenate([
            jnp.dot(seqh[h, pl.ds(pl.multiple_of(c * 128, 128), 128), :], w, preferred_element_type=F32),
            jnp.dot(seqh[h, pl.ds(pl.multiple_of((1 - c) * 128, 128), 128), :], w, preferred_element_type=F32),
        ], axis=0)

    part = project(c)
    half_copy.wait_recv()
    proj = (part + project(1 - c)).astype(BF16)
    kv[z] = proj[:, 256:640]

    kv_right, kv_left, pair_copies = {}, {}, {}

    def to_pair(name, zo):
        pair_copies[name] = (
            remote(kv.at[zo, 0:64, 0:256], c2.at[zo, :, 0:256], x_pair),
            remote(kv.at[zo, 64:128, 256:384], c2.at[zo, :, 256:384], x_pair),
        )

    kv_right[0] = remote(kv.at[z], kv.at[z], right)
    kv_left[0] = remote(kv.at[z], kv.at[z], left)
    to_pair(0, z)

    lane256 = iota((256, 128), 1)
    q01 = proj[:, 0:128].astype(F32)
    q2 = proj[:, 128:256].astype(F32)
    qm[0] = jnp.where(lane256 < 64, q01, 0.0).astype(BF16)
    qm[1] = jnp.where(lane256 < 64, 0.0, q01).astype(BF16)
    qm[2] = jnp.where(lane256 < 64, q2, 0.0).astype(BF16)

    rr, cc = iota((256, 256), 0), iota((256, 256), 1)
    both = jnp.where((rr < 128) & (cc < 128), 2.0, 1.0)
    mask_s[0] = both + jnp.where((rr < 64) & (cc < 64), 1.0, 0.0)
    mask_s[1] = both + jnp.where((rr >= 64) & (rr < 128) & (cc >= 64) & (cc < 128), 1.0, 0.0)

    key_cols = (0, 0, 256)
    value_cols = (128, 128, 256)

    def update(h, lo, rows, keys, values, mult, fresh=False):
        at = pl.ds(lo, rows)
        s = nt_dot(qm[h, at, :], keys)
        top = jnp.max(s, axis=1, keepdims=True)
        if fresh:
            m_new = top
        else:
            m_old = m_s[h, at, :]
            m_new = jnp.maximum(m_old, top)
            keep = jnp.exp2((m_old - m_new) * EXP2_SCALE)
        p = jnp.exp2((s - m_new) * EXP2_SCALE)
        if mult is not None:
            p = p * mult
        total_p = jnp.sum(p, axis=1, keepdims=True)
        pv = jnp.dot(p.astype(BF16), values, preferred_element_type=F32)
        m_s[h, at, :] = m_new
        if fresh:
            l_s[h, at, :] = total_p
            acc_s[h, at, :] = pv
        else:
            l_s[h, at, :] = l_s[h, at, :] * keep + total_p
            acc_s[h, at, :] = acc_s[h, at, :] * keep + pv

    def full_block(zo, fresh=False):
        for h in range(3):
            update(
                h, 0, 256, kv[zo, :, key_cols[h] : key_cols[h] + 128],
                kv[zo, :, value_cols[h] : value_cols[h] + 128], mask_s[h // 2], fresh,
            )

    def part_block(zo):
        for h in range(3):
            update(
                h, 0, 128, kv[zo, 0:128, key_cols[h] : key_cols[h] + 128],
                kv[zo, 0:128, value_cols[h] : value_cols[h] + 128],
                mask_s[h // 2, 0:128, 0:128] - 1.0,
            )

    def attend(zo):
        same = zo // 4 == z // 4

        @pl.when(same)
        def _():
            full_block(zo)

        @pl.when(jnp.logical_not(same))
        def _():
            part_block(zo)

    full_block(z, fresh=True)
    for s in (1, 2, 3):
        zr, zl = (z - s) % NZ, (z + s) % NZ
        kv_right[s - 1].wait_recv()
        if s < 3:
            kv_right[s] = remote(kv.at[zr], kv.at[zr], right)
        else:
            kv_right[s] = remote(kv.at[zr, 0:128], kv.at[zr, 0:128], right)
        kv_left[s - 1].wait_recv()
        if s < 3:
            kv_left[s] = remote(kv.at[zl], kv.at[zl], left)
        to_pair(("r", s), zr)
        to_pair(("l", s), zl)
        attend(zr)
        attend(zl)
    kv_right[3].wait_recv()
    z_far = (z + 4) % NZ
    to_pair("far", z_far)
    part_block(z_far)
    for copies in pair_copies.values():
        for copy in copies:
            copy.wait_recv()
    for h in range(3):
        update(
            h, 64 * (h // 2), 64,
            c2[:, :, key_cols[h] : key_cols[h] + 128].reshape(512, 128),
            c2[:, :, value_cols[h] : value_cols[h] + 128].reshape(512, 128), None,
        )

    heads = [acc_s[h] / l_s[h] for h in range(3)]
    done = jnp.concatenate(
        [jnp.where(lane256 < 64, heads[0], heads[1]), heads[2]], axis=1
    ).astype(BF16)
    p_row, n_col = iota((128, 256), 0), iota((128, 256), 1)

    def arranged(oc):
        res = p_row % 4
        source = jnp.where(res % 2 == c, 0, 128) + (res // 2) * 64 + oc * 32 + p_row // 4
        hot = (n_col == source).astype(F32).astype(BF16)
        rows = jnp.dot(hot, done, preferred_element_type=F32)
        a, b = rows[:, 0:128], rows[:, 128:256]
        a_rolled, b_rolled = roll64(a), roll64(b)
        return jnp.concatenate([
            jnp.where(c == 0, a, a_rolled),
            jnp.where(c == 0, b_rolled, b),
            jnp.where(c == 0, a_rolled, a),
        ], axis=1)

    fin[0] = arranged(1 - c).astype(BF16)
    fin_copy = remote(fin.at[0], fin.at[1], sibling)
    mine = arranged(c)
    fin_copy.wait_recv()
    own_lane = (iota((128, HALF), 1) // 64) % 2 == c
    out_ref[...] = jnp.where(own_lane, mine, fin[1].astype(F32)).astype(BF16)

    for copy in started:
        copy.wait_send()


def local(tile_embeddings, tile_position, input_weight, attention_weight):
    vmem = pl.BlockSpec(memory_space=pltpu.VMEM)
    anywhere = pl.BlockSpec(memory_space=pl.ANY)
    scratch = [
        pltpu.VMEM((SLOTS, E), BF16),
        pltpu.VMEM((SLOTS, E), BF16),
        pltpu.VMEM((1, SLOTS), jnp.int32),
        pltpu.VMEM((W_ROWS, HALF), BF16),
        pltpu.VMEM((NX, NZ, 2 * W_ROWS, HALF), BF16),
        pltpu.VMEM((D, 1152), BF16),
        pltpu.VMEM((D, 640), BF16),
        pltpu.VMEM((NX, NZ, 128), F32),
        pltpu.VMEM((NX, NZ, 128), F32),
        pltpu.VMEM((NZ, 8, 128), F32),
        pltpu.VMEM((NZ, 8, 128), F32),
        pltpu.VMEM((2 * SLOTS, HALF), BF16),
        pltpu.VMEM((NX, NZ, 32, HALF), BF16),
        pltpu.VMEM((NZ, NX, 32, HALF), BF16),
        pltpu.VMEM((3, NZ, 32, HALF), BF16),
        pltpu.VMEM((NZ, 256, HALF), BF16),
        pltpu.VMEM((NZ, 64, HALF), BF16),
        pltpu.VMEM((3, 256, 128), BF16),
        pltpu.VMEM((3, 256, 1), F32),
        pltpu.VMEM((3, 256, 1), F32),
        pltpu.VMEM((3, 256, 128), F32),
        pltpu.VMEM((2, 256, 256), F32),
        pltpu.VMEM((2, 128, HALF), BF16),
        pltpu.VMEM((2, 256, HALF), BF16),
        pltpu.SemaphoreType.DMA((N_COPIES,)),
        pltpu.SemaphoreType.DMA((N_COPIES,)),
        pltpu.SemaphoreType.DMA((2,)),
    ]
    return pl.pallas_call(
        kernel,
        out_shape=jax.ShapeDtypeStruct((TOK_DEV, HALF), BF16),
        in_specs=[anywhere, vmem, vmem, anywhere],
        out_specs=vmem,
        scratch_shapes=scratch,
        compiler_params=pltpu.CompilerParams(
            collective_id=0, has_side_effects=True, vmem_limit_bytes=48 * 1024 * 1024
        ),
    )(tile_embeddings, tile_position.reshape(1, SLOTS), input_weight, attention_weight)


def solution(mesh):
    in_specs = (P(("slide", "seq"), None), P(("slide", "seq")), P("seq", None), P())
    out_specs = P(("slide", "seq"), None)
    return jax.shard_map(local, mesh=mesh, in_specs=in_specs, out_specs=out_specs, check_vma=False)
```

time: 292 us -> 96.2 us (0.33)
  waiting for transfers between devices: 107 us -> 0 us
  Pallas kernels: 0 us -> 91.3 us
  starting transfers between devices: 91.2 us -> 0 us
  other arithmetic: 35.8 us -> 0 us
  local copies, waits for them, and re-layouts: 23.7 us -> 4.7 us
  matrix products: 17.7 us -> 0 us
  between operations: 14.3 us -> 0.01 us
    pallas_call x0 -> x1, Pallas kernels: none -> 91.3 us  [local(): pl.pallas_call(kernel, out_shape=jax.ShapeDtypeStruct((TOK_DEV, HALF), BF...]
    ppermute x24 -> x0, starting transfers between devices: 71.4 us -> none  [from_partner(): return lax.ppermute(value, axis, pairs)]
    all_to_all x2 -> x0, waiting for transfers between devices: 46 us -> none  [the longest x1 40.5 us: local(): lax.all_to_all(outgoing.reshape(devices, per_neighbor, -1), 'seq', split_...]
    ppermute x24 -> x0, waiting for transfers between devices: 44.1 us -> none  [from_partner(): return lax.ppermute(value, axis, pairs)]
    select_n x37 -> x0, other arithmetic: 32.2 us -> none  [the longest x33 30.8 us: widen_group(): jnp.where(is_lower, jnp.concatenate([own_part, theirs], 0), jnp.concatena...]
    all_to_all x2 -> x0, starting transfers between devices: 19.8 us -> none  [the longest x1 14.8 us: local(): lax.all_to_all(spot_marks, 'seq', split_axis=0, concat_axis=0, tiled=True)]
    dot_general x9 -> x0, matrix products: 17.7 us -> none  [the longest x3 7.03 us: local(): jnp.einsum('hqk,khd->hqd', weights.astype(jnp.bfloat16), near_values, pre...]
    all_gather x1 -> x0, waiting for transfers between devices: 15.8 us -> none  [project(): lax.all_gather(input_weight, 'seq', axis=0, tiled=True)]
  transfers between devices with their start and end apart: 27 -> 0, of which waited for: 5 -> 0; matrix products, arithmetic and copies ran while one was open for 24% -> 0% of each run, Pallas kernels for 0% -> 0%
where the time goes in v1:
time: 96.2 us; the launch traced here: 96 us
  Pallas kernels  91.3 us (95%)
  local copies, waits for them, and re-layouts  4.7 us (5%)
    pallas_call x1, Pallas kernels, local(): pl.pallas_call(kernel, out_shape=jax.ShapeDtypeStruct((TOK_DEV, HALF), BF...  91.3 us
    unnamed x9, local copies, waits for them, and re-layouts  4.7 us

profile of v1, /device:TPU:1, one launch (start us, length us, event | category | flops | bytes accessed | tf_op | source)
XLA Modules:
  0.0 96.0 jit_solution(8129133676771480466)
XLA Ops:
  0.0 0.0 copy-start
  0.0 1.5 %copy-done = bf16[768,1152]{1,0:T(8,128)(2,1)S(1)} copy-done((bf16[768,1152]{1,0:T(8,128)(2,1)S(1)}, bf16[768,1152]{1,0:T(8,128)(2,1)}, u32[]{:S(2)}) %copy-start) | copy-done | bytes 1769496
  1.5 0.0 copy-start.1
  1.5 1.1 %copy-done.1 = bf16[256,1536]{1,0:T(8,128)(2,1)S(1)} copy-done((bf16[256,1536]{1,0:T(8,128)(2,1)S(1)}, bf16[256,1536]{1,0:T(8,128)(2,1)}, u32[]{:S(2)}) %copy-start.1) | copy-done | bytes 786456
  2.6 0.0 copy-start.2
  2.6 0.8 copy-done.2
  3.4 0.0 copy-start.3
  3.4 0.7 copy-done.3
  4.1 91.3 %shard_map.46 = bf16[128,384]{1,0:T(8,128)(2,1)S(1)} custom-call(bf16[256,1536]{1,0:T(8,128)(2,1)S(1)} %copy-done.1, s32[1,256]{1,0:T(1,128)S(1)} %bitcast.1, bf16[24,768]{1,0:T(8,128)(2,1)S(1)} %copy-done.2, bf16[768,1152]{1,0:T(8,128)(2,1)S(1)} %copy-done), custom_call_target="tpu_custom_call" | custom-call | tf_op jit(solution)/shard_map/pallas_call | solution.py:401
  95.3 0.6 copy.6
Async XLA Ops:
  0.0 1.5 %copy-start = (bf16[768,1152]{1,0:T(8,128)(2,1)S(1)}, bf16[768,1152]{1,0:T(8,128)(2,1)}, u32[]{:S(2)}) copy-start(bf16[768,1152]{1,0:T(8,128)(2,1)} %aw_ref.1) | copy-start | bytes 5308420
  1.5 1.1 %copy-start.1 = (bf16[256,1536]{1,0:T(8,128)(2,1)S(1)}, bf16[256,1536]{1,0:T(8,128)(2,1)}, u32[]{:S(2)}) copy-start(bf16[256,1536]{1,0:T(8,128)(2,1)} %emb_ref.1) | copy-start | bytes 2359300
  2.6 0.8 copy-start.2
  3.4 0.7 copy-start.3

commit v2 on v1

--- a/solution.py
+++ b/solution.py
@@ -33,15 +33,17 @@
     return jnp.concatenate([a[:, 64:], a[:, :64]], axis=1)
 
 
-N_COPIES = 160
+N_COPIES = 230
+N_W = 70
 
 
 def kernel(
-    emb_ref, pos_ref, w_ref, aw_ref, out_ref,
-    emb_own, emb_sib, pos_sib, w_sib, wbuf, awbuf, awc,
+    emb_in, pos_in, w_in, aw_in, out_ref,
+    pos_ref, w_ref,
+    emb_own, emb_sib, pos_sib, wbuf, awbuf, awc,
     marks, marks_mid, marks_z, marks_got,
-    seq, mid, got, xout, kv, c2, qm, m_s, l_s, acc_s, mask_s, fin, seqh,
-    send_sems, recv_sems, local_sems,
+    hot_s, seq, mid, got, xout, kv, c2, qm, m_s, l_s, acc_s, mask_s, fin, seqh,
+    send_sems, recv_sems, w_sems, local_sems,
 ):
     me = lax.axis_index("seq")
     slide = lax.axis_index("slide")
@@ -57,47 +59,120 @@
     x_pair = dev(x + 1 - 2 * (x % 2), z, c)
 
     started = []
-
-    def remote(src, dst, target):
+    w_names = {}
+
+    def remote(src, dst, target, when=None, recv_sem=None):
         k = len(started)
         copy = pltpu.make_async_remote_copy(
-            src_ref=src, dst_ref=dst, send_sem=send_sems.at[k], recv_sem=recv_sems.at[k],
+            src_ref=src, dst_ref=dst, send_sem=send_sems.at[k],
+            recv_sem=recv_sems.at[k] if recv_sem is None else recv_sem,
             device_id=target, device_id_type=MESH,
         )
-        started.append(copy)
-        copy.start()
+        started.append((copy, when))
+        if when is None:
+            copy.start()
+        else:
+            pl.when(when)(copy.start)
         return copy
 
-    emb_load = pltpu.make_async_copy(emb_ref, emb_own, local_sems.at[0])
-    emb_load.start()
-    aw_load = pltpu.make_async_copy(aw_ref, awbuf, local_sems.at[1])
-    aw_load.start()
+    w_load = pltpu.make_async_copy(w_in, w_ref, local_sems.at[0])
+    pos_load = pltpu.make_async_copy(pos_in, pos_ref, local_sems.at[1])
+    emb_load = pltpu.make_async_copy(emb_in, emb_own, local_sems.at[2])
+    aw_load = pltpu.make_async_copy(aw_in, awbuf, local_sems.at[3])
+    for load in (w_load, pos_load, emb_load, aw_load):
+        load.start()
 
     barrier = pltpu.get_barrier_semaphore()
     partners = [sibling] + [dev(x_of[d], z, c) for d in (1, 2, 3)] + [dev(x, z_of[d], c) for d in range(1, 8)]
+    partners += [dev(x_of[d], z, 1 - c) for d in (1, 2, 3)] + [dev(x, z_of[d], 1 - c) for d in (1, 4, 7)]
     for partner in partners:
         pl.semaphore_signal(barrier, inc=1, device_id=partner, device_id_type=MESH)
     pl.semaphore_wait(barrier, len(partners))
 
-    w_copy = remote(w_ref.at[:, pl.ds(pl.multiple_of((1 - c) * HALF, 128), HALF)], w_sib, sibling)
+    w_load.wait()
+
+    def w_half(h):
+        return w_ref.at[:, pl.ds(pl.multiple_of(h * HALF, 128), HALF)]
+
+    own_slot = wbuf.at[x, z, c]
+
+    def w_sem(name, core):
+        k = w_names.setdefault(name, len(w_names))
+        return w_sems.at[2 * k + core]
+
+    def w_give(name, target_x, target_z, when=None):
+        for half in (c, 1 - c):
+            remote(w_half(half), own_slot, dev(target_x, target_z, half), when, w_sem(name, c))
+
+    def w_take(name, xo, zo, core):
+        slot = wbuf.at[xo, zo, core]
+        pltpu.make_async_remote_copy(
+            src_ref=slot, dst_ref=slot, send_sem=send_sems.at[0], recv_sem=w_sem(name, core),
+            device_id=sibling, device_id_type=MESH,
+        ).wait_recv()
+        return slot
+
+    w_give(("z", 1), x, z_of[1])
+    w_give(("z", 7), x, z_of[7])
+    w_give(("z", 4), x, z_of[4], c == 1)
+    for d in (1, 3, 2):
+        w_give(("x", d), x_of[d], z)
+    remote(w_half(1 - c), own_slot, sibling, None, w_sem("cross", c))
+    pos_load.wait()
     pos_copy = remote(pos_ref, pos_sib, sibling)
     emb_load.wait()
     emb_copy = remote(emb_own, emb_sib, sibling)
-
-    w_copy.wait_recv()
-    w_mine = w_ref[:, pl.ds(pl.multiple_of(c * HALF, 128), HALF)].astype(F32)
-    w_theirs = w_sib[...].astype(F32)
-    first = jnp.where(c == 0, w_mine, w_theirs)
-    second = jnp.where(c == 0, w_theirs, w_mine)
-    wbuf[x, z] = jnp.concatenate([first, second], axis=0).astype(BF16)
-
-    w_x = {}
-    w_right, w_left = {}, {}
-    own_block = wbuf.at[x, z]
-    for d in (1, 3, 2):
-        w_x[d] = remote(own_block, own_block, dev(x_of[d], z, c))
-    w_right[0, 0] = remote(own_block, own_block, right)
-    w_left[0, 0] = remote(own_block, own_block, left)
+    wbuf[x, z, c] = w_ref[:, pl.ds(pl.multiple_of(c * HALF, 128), HALF)]
+
+    def w_send(name, slot, xx, zz, core):
+        remote(slot, slot, dev(xx, zz, c), None, w_sem(name, core))
+
+    def w_along_x(e, slot):
+        for d in (1, 3, 2):
+            w_send(("zx", e, d), slot, x_of[d], z, 1)
+
+    def w_ring(way, s, d):
+        if s == 0 and d == 0:
+            return ("z", 1) if way == 0 else ("z", 7)
+        return ("ring", way, s, d)
+
+    def w_ring_step(s):
+        for d in (0, 1, 3, 2):
+            xo = (x - d) % NX
+            for way in (0, 1):
+                if s > (4, 3)[way]:
+                    continue
+                zo = (z - s) % NZ if way == 0 else (z + s) % NZ
+                slot = w_take(w_ring(way, s - 1, d), xo, zo, 0)
+                if s < (4, 3)[way]:
+                    w_send(w_ring(way, s, d), slot, x, z_of[(1, 7)[way]], 0)
+
+    aw_load.wait()
+    lane = iota((D, 128), 1)
+
+    def pair(group_a, group_b):
+        a = awbuf[:, group_a * 128 : group_a * 128 + 128].astype(F32)
+        b = awbuf[:, group_b * 128 : group_b * 128 + 128].astype(F32)
+        even = jnp.where(lane < 64, a, roll64(b))
+        odd = jnp.where(lane < 64, roll64(a), b)
+        return jnp.where(c == 0, even, odd).astype(BF16)
+
+    awc[:, 0:128] = pair(0, 2)
+    awc[:, 128:256] = pair(1, 1)
+    awc[:, 256:384] = pair(3, 5)
+    awc[:, 384:512] = pair(6, 8)
+    awc[:, 512:640] = pair(4, 7)
+
+    for d in (1, 3, 2):
+        xo = (x - d) % NX
+        slot = w_take(("x", d), xo, z, 0)
+        for way in (0, 1):
+            w_send(w_ring(way, 0, d), slot, x, z_of[(1, 7)[way]], 0)
+    for e, onward in ((1, ((7, 2),)), (7, ((1, 6),)), (4, ((1, 3), (7, 5)))):
+        slot = w_take(("z", 8 - e), x, z_of[e], 1)
+        for to, seen in onward:
+            w_send(("far", seen), slot, x, z_of[to], 1)
+        w_along_x(e, slot)
 
     pos_copy.wait_recv()
     pos = jnp.concatenate([pos_ref[...], pos_sib[...]], axis=1)
@@ -126,12 +201,9 @@
     for d in (1, 3, 2):
         mark_x[d] = remote(marks.at[x_of[d]], marks_mid.at[x], dev(x_of[d], z, c))
 
-    for d in (1, 3, 2):
-        w_x[d].wait_recv()
-        xo = (x - d) % NX
-        block = wbuf.at[xo, z]
-        w_right[0, d] = remote(block, block, right)
-        w_left[0, d] = remote(block, block, left)
+    w_ring_step(1)
+    for e in (2, 6, 3, 5):
+        w_along_x(e, w_take(("far", e), x, z_of[e], 1))
 
     for d in (1, 3, 2):
         mark_x[d].wait_recv()
@@ -146,35 +218,17 @@
     for d in range(1, NZ):
         mark_z[d] = remote(marks_z.at[z_of[d]], marks_got.at[z], dev(x, z_of[d], c))
 
-    aw_load.wait()
-    lane = iota((D, 128), 1)
-
-    def pair(group_a, group_b):
-        a = awbuf[:, group_a * 128 : group_a * 128 + 128].astype(F32)
-        b = awbuf[:, group_b * 128 : group_b * 128 + 128].astype(F32)
-        even = jnp.where(lane < 64, a, roll64(b))
-        odd = jnp.where(lane < 64, roll64(a), b)
-        return jnp.where(c == 0, even, odd).astype(BF16)
-
-    awc[:, 0:128] = pair(0, 2)
-    awc[:, 128:256] = pair(1, 1)
-    awc[:, 256:384] = pair(3, 5)
-    awc[:, 384:512] = pair(6, 8)
-    awc[:, 512:640] = pair(4, 7)
-
-    for s in (1, 2, 3):
-        for d in (0, 1, 3, 2):
-            xo = (x - d) % NX
-            w_right[s - 1, d].wait_recv()
-            block = wbuf.at[xo, (z - s) % NZ]
-            w_right[s, d] = remote(block, block, right)
-            if s <= 2:
-                w_left[s - 1, d].wait_recv()
-                block = wbuf.at[xo, (z + s) % NZ]
-                w_left[s, d] = remote(block, block, left)
-    for d in (0, 1, 3, 2):
-        w_left[2, d].wait_recv()
-        w_right[3, d].wait_recv()
+    for d in range(NX):
+        rows = iota((256, slots), 0) + x_of[d] * 256
+        hot_s[d] = (rows.astype(F32) == target_row).astype(F32).astype(BF16)
+
+    for s in (2, 3, 4):
+        w_ring_step(s)
+    w_take("cross", x, z, 1 - c)
+    for d in (1, 3, 2):
+        w_take(("x", d), (x - d) % NX, z, 1)
+        for e in range(1, NZ):
+            w_take(("zx", e, d), (x - d) % NX, z_of[e], 1)
 
     weight = wbuf[...].reshape(E, HALF)
     seq[0:SLOTS] = jnp.dot(emb_own[...], weight, preferred_element_type=F32).astype(BF16)
@@ -184,22 +238,27 @@
     out_x = {}
     z_sent = {}
 
-    def rows_for(xo):
-        hot = (iota((256, slots), 0) + xo * 256).astype(F32) == target_row
-        rows = jnp.dot(hot.astype(F32).astype(BF16), seq[...], preferred_element_type=F32)
+    def rows_for(d):
+        rows = jnp.dot(hot_s[d], seq[...], preferred_element_type=F32)
         return rows.astype(BF16).reshape(NZ, 32, HALF)
 
-    mid[x] = rows_for(x)
-    for d in (4, 3, 5, 2, 6, 1, 7):
-        z_sent[0, d] = remote(mid.at[x, z_of[d]], got.at[z, x], dev(x, z_of[d], c))
-    for d in (2, 1, 3):
-        xout[d - 1] = rows_for(x_of[d])
+    def send_x(d):
+        xout[d - 1] = rows_for(d)
         out_x[d] = remote(xout.at[d - 1], mid.at[x], dev(x_of[d], z, c))
-    for d in (1, 3, 2):
-        out_x[d].wait_recv()
+
+    def send_z(d):
         xo = (x - d) % NX
         for e in (4, 3, 5, 2, 6, 1, 7):
             z_sent[d, e] = remote(mid.at[xo, z_of[e]], got.at[z, xo], dev(x, z_of[e], c))
+
+    send_x(1)
+    send_x(3)
+    mid[x] = rows_for(0)
+    send_z(0)
+    send_x(2)
+    for d in (1, 3, 2):
+        out_x[d].wait_recv()
+        send_z(d)
 
     row = iota((256, 128), 0)
     group = row // 64
@@ -231,17 +290,46 @@
     proj = (part + project(1 - c)).astype(BF16)
     kv[z] = proj[:, 256:640]
 
-    kv_right, kv_left, pair_copies = {}, {}, {}
-
-    def to_pair(name, zo):
-        pair_copies[name] = (
-            remote(kv.at[zo, 0:64, 0:256], c2.at[zo, :, 0:256], x_pair),
-            remote(kv.at[zo, 64:128, 256:384], c2.at[zo, :, 256:384], x_pair),
-        )
-
-    kv_right[0] = remote(kv.at[z], kv.at[z], right)
-    kv_left[0] = remote(kv.at[z], kv.at[z], left)
-    to_pair(0, z)
+    in_seg = (z % 4, 3 - z % 4)
+    pair_copies = []
+    flow = {}
+
+    def low_sent(i, s):
+        return None if s < 3 else (i == 3) | (i == 0)
+
+    def low_got(i, s):
+        return None if s < 3 else (i == 0) | (i == 1)
+
+    def rest_sent(i, s):
+        return (i >= s) & (i <= 2)
+
+    def rest_got(i, s):
+        return i >= s + 1
+
+    def origin(way, s):
+        return (z - s) % NZ if way == 0 else (z + s) % NZ
+
+    def pass_on(way, part, s, k):
+        sent = low_sent if part == "low" else rest_sent
+        block = kv.at[origin(way, s), pl.ds(k * 64 + (0 if part == "low" else 128), 64)]
+        flow[way, part, s, k] = remote(block, block, (right, left)[way], sent(in_seg[way], s))
+
+    def wait_for(copy, when):
+        if when is None:
+            copy.wait_recv()
+        else:
+            pl.when(when)(copy.wait_recv)
+
+    def to_pair(zo, when=None):
+        for rows, cols in ((0, slice(0, 256)), (64, slice(256, 384))):
+            copy = remote(kv.at[zo, rows : rows + 64, cols], c2.at[zo, :, cols], x_pair, when)
+            pair_copies.append((copy, when))
+
+    for part in ("low", "rest"):
+        for k in (0, 1):
+            for way in (0, 1):
+                pass_on(way, part, 0, k)
+    to_pair(z)
 
     lane256 = iota((256, 128), 1)
     q01 = proj[:, 0:128].astype(F32)
@@ -296,45 +384,45 @@
                 mask_s[h // 2, 0:128, 0:128] - 1.0,
             )
 
-    def attend(zo):
-        same = zo // 4 == z // 4
-
-        @pl.when(same)
-        def _():
-            full_block(zo)
-
-        @pl.when(jnp.logical_not(same))
-        def _():
-            part_block(zo)
+    def pair_block(copies, offsets):
+        for copy, when in copies:
+            wait_for(copy, when)
+        blocks = [c2[z_of[e]] for e in offsets]
+        block = jnp.concatenate(blocks, axis=0)
+        for h in range(3):
+            update(
+                h, 64 * (h // 2), 64, block[:, key_cols[h] : key_cols[h] + 128],
+                block[:, value_cols[h] : value_cols[h] + 128], None,
+            )
 
     full_block(z, fresh=True)
-    for s in (1, 2, 3):
-        zr, zl = (z - s) % NZ, (z + s) % NZ
-        kv_right[s - 1].wait_recv()
+    for s in range(4):
+        for k in (0, 1):
+            for way in (0, 1):
+                wait_for(flow[way, "low", s, k], low_got(in_seg[way], s))
+                if s < 3:
+                    pass_on(way, "low", s + 1, k)
+        for way in (0, 1):
+            to_pair(origin(way, s + 1), low_got(in_seg[way], s))
         if s < 3:
-            kv_right[s] = remote(kv.at[zr], kv.at[zr], right)
-        else:
-            kv_right[s] = remote(kv.at[zr, 0:128], kv.at[zr, 0:128], right)
-        kv_left[s - 1].wait_recv()
-        if s < 3:
-            kv_left[s] = remote(kv.at[zl], kv.at[zl], left)
-        to_pair(("r", s), zr)
-        to_pair(("l", s), zl)
-        attend(zr)
-        attend(zl)
-    kv_right[3].wait_recv()
-    z_far = (z + 4) % NZ
-    to_pair("far", z_far)
-    part_block(z_far)
-    for copies in pair_copies.values():
-        for copy in copies:
-            copy.wait_recv()
-    for h in range(3):
-        update(
-            h, 64 * (h // 2), 64,
-            c2[:, :, key_cols[h] : key_cols[h] + 128].reshape(512, 128),
-            c2[:, :, value_cols[h] : value_cols[h] + 128].reshape(512, 128), None,
-        )
+            for k in (0, 1):
+                for way in (0, 1):
+                    pl.when(rest_got(in_seg[way], s))(flow[way, "rest", s, k].wait_recv)
+                    if s < 2:
+                        pass_on(way, "rest", s + 1, k)
+        if s == 3:
+            pair_block(pair_copies[:10], (0, 7, 1, 6, 2))
+        for way in (0, 1):
+            zo = origin(way, s + 1)
+            got_low = low_got(in_seg[way], s)
+            if s < 3:
+                full = rest_got(in_seg[way], s)
+                pl.when(full)(lambda: full_block(zo))
+                part = jnp.logical_not(full)
+                pl.when(part if got_low is None else part & got_low)(lambda: part_block(zo))
+            else:
+                pl.when(got_low)(lambda: part_block(zo))
+    pair_block(pair_copies[10:], (3, 5, 4))
 
     heads = [acc_s[h] / l_s[h] for h in range(3)]
     done = jnp.concatenate(
@@ -362,25 +450,30 @@
     own_lane = (iota((128, HALF), 1) // 64) % 2 == c
     out_ref[...] = jnp.where(own_lane, mine, fin[1].astype(F32)).astype(BF16)
 
-    for copy in started:
-        copy.wait_send()
+    for copy, when in started:
+        if when is None:
+            copy.wait_send()
+        else:
+            pl.when(when)(copy.wait_send)
 
 
 def local(tile_embeddings, tile_position, input_weight, attention_weight):
     vmem = pl.BlockSpec(memory_space=pltpu.VMEM)
     anywhere = pl.BlockSpec(memory_space=pl.ANY)
     scratch = [
+        pltpu.VMEM((1, SLOTS), jnp.int32),
+        pltpu.VMEM((W_ROWS, 2 * HALF), BF16),
         pltpu.VMEM((SLOTS, E), BF16),
         pltpu.VMEM((SLOTS, E), BF16),
         pltpu.VMEM((1, SLOTS), jnp.int32),
-        pltpu.VMEM((W_ROWS, HALF), BF16),
-        pltpu.VMEM((NX, NZ, 2 * W_ROWS, HALF), BF16),
+        pltpu.VMEM((NX, NZ, 2, W_ROWS, HALF), BF16),
         pltpu.VMEM((D, 1152), BF16),
         pltpu.VMEM((D, 640), BF16),
         pltpu.VMEM((NX, NZ, 128), F32),
         pltpu.VMEM((NX, NZ, 128), F32),
         pltpu.VMEM((NZ, 8, 128), F32),
         pltpu.VMEM((NZ, 8, 128), F32),
+        pltpu.VMEM((NX, 256, 2 * SLOTS), BF16),
         pltpu.VMEM((2 * SLOTS, HALF), BF16),
         pltpu.VMEM((NX, NZ, 32, HALF), BF16),
         pltpu.VMEM((NZ, NX, 32, HALF), BF16),
@@ -396,16 +489,17 @@
         pltpu.VMEM((2, 256, HALF), BF16),
         pltpu.SemaphoreType.DMA((N_COPIES,)),
         pltpu.SemaphoreType.DMA((N_COPIES,)),
-        pltpu.SemaphoreType.DMA((2,)),
+        pltpu.SemaphoreType.DMA((2 * N_W,)),
+        pltpu.SemaphoreType.DMA((4,)),
     ]
     return pl.pallas_call(
         kernel,
         out_shape=jax.ShapeDtypeStruct((TOK_DEV, HALF), BF16),
-        in_specs=[anywhere, vmem, vmem, anywhere],
+        in_specs=[anywhere] * 4,
         out_specs=vmem,
         scratch_shapes=scratch,
         compiler_params=pltpu.CompilerParams(
-            collective_id=0, has_side_effects=True, vmem_limit_bytes=48 * 1024 * 1024
+            collective_id=0, has_side_effects=True, vmem_limit_bytes=60 * 1024 * 1024
         ),
     )(tile_embeddings, tile_position.reshape(1, SLOTS), input_weight, attention_weight)
 

time: 96.2 us -> 83.7 us (0.87)
  Pallas kernels: 91.3 us -> 82 us
  local copies, waits for them, and re-layouts: 4.7 us -> 1.54 us
    pallas_call x1, Pallas kernels: 91.3 us -> 82 us  [local(): pl.pallas_call(kernel, out_shape=jax.ShapeDtypeStruct((TOK_DEV, HALF), BF...]
    unnamed x9 -> x1, local copies, waits for them, and re-layouts: 4.7 us -> 1.54 us
where the time goes in v2:
time: 83.7 us; the launch traced here: 83.5 us
  Pallas kernels  82 us (98%)
  local copies, waits for them, and re-layouts  1.54 us (2%)
    pallas_call x1, Pallas kernels, local(): pl.pallas_call(kernel, out_shape=jax.ShapeDtypeStruct((TOK_DEV, HALF), BF...  82 us

profile of v2, /device:TPU:1, one launch (start us, length us, event | category | flops | bytes accessed | tf_op | source)
XLA Modules:
  0.0 83.5 jit_solution(2747567285564794682)
XLA Ops:
  0.0 82.0 %shard_map.46 = bf16[128,384]{1,0:T(8,128)(2,1)} custom-call(bf16[256,1536]{1,0:T(8,128)(2,1)} %emb_in.1, s32[1,256]{1,0:T(1,128)} %bitcast.1, bf16[24,768]{1,0:T(8,128)(2,1)} %w_in.1, bf16[768,1152]{1,0:T(8,128)(2,1)} %aw_in.1), custom_call_target="tpu_custom_call" | custom-call | tf_op jit(solution)/shard_map/pallas_call | solution.py:495
  82.0 1.5 %copy.6 = bf16[128,384]{1,0:T(8,128)(2,1)} copy(bf16[128,384]{1,0:T(8,128)(2,1)} %shard_map.46) | data formatting | bytes 196608

commit v3 on v2

--- a/solution.py
+++ b/solution.py
@@ -33,8 +33,7 @@
     return jnp.concatenate([a[:, 64:], a[:, :64]], axis=1)
 
 
-N_COPIES = 230
-N_W = 70
+N_SEMS = 100
 
 
 def kernel(
@@ -43,7 +42,7 @@
     emb_own, emb_sib, pos_sib, wbuf, awbuf, awc,
     marks, marks_mid, marks_z, marks_got,
     hot_s, seq, mid, got, xout, kv, c2, qm, m_s, l_s, acc_s, mask_s, fin, seqh,
-    send_sems, recv_sems, w_sems, local_sems,
+    sems, local_sems,
 ):
     me = lax.axis_index("seq")
     slide = lax.axis_index("slide")
@@ -58,22 +57,36 @@
     right, left = dev(x, z_of[1], c), dev(x, z_of[7], c)
     x_pair = dev(x + 1 - 2 * (x % 2), z, c)
 
-    started = []
-    w_names = {}
-
-    def remote(src, dst, target, when=None, recv_sem=None):
-        k = len(started)
+    names = {}
+
+    def sem(name):
+        return sems.at[names.setdefault(name, len(names))]
+
+    def guarded(when, action):
+        if when is None:
+            action()
+        else:
+            pl.when(when)(action)
+
+    def put(src, dst, target, sent_as, got_as, when=None):
         copy = pltpu.make_async_remote_copy(
-            src_ref=src, dst_ref=dst, send_sem=send_sems.at[k],
-            recv_sem=recv_sems.at[k] if recv_sem is None else recv_sem,
+            src_ref=src, dst_ref=dst, send_sem=sem(("sent", sent_as)), recv_sem=sem(got_as),
             device_id=target, device_id_type=MESH,
         )
-        started.append((copy, when))
-        if when is None:
-            copy.start()
-        else:
-            pl.when(when)(copy.start)
-        return copy
+        guarded(when, copy.start)
+
+    def bytes_of(ref, name):
+        return pltpu.make_async_remote_copy(
+            src_ref=ref, dst_ref=ref, send_sem=sem(name), recv_sem=sem(name),
+            device_id=sibling, device_id_type=MESH,
+        )
+
+    def take(ref, name, when=None):
+        guarded(when, bytes_of(ref, name).wait_recv)
+        return ref
+
+    def sent(ref, name, when=None):
+        guarded(when, bytes_of(ref, ("sent", name)).wait_send)
 
     w_load = pltpu.make_async_copy(w_in, w_ref, local_sems.at[0])
     pos_load = pltpu.make_async_copy(pos_in, pos_ref, local_sems.at[1])
@@ -96,56 +109,36 @@
 
     own_slot = wbuf.at[x, z, c]
 
-    def w_sem(name, core):
-        k = w_names.setdefault(name, len(w_names))
-        return w_sems.at[2 * k + core]
-
-    def w_give(name, target_x, target_z, when=None):
+    def w_give(kind, d, target_x, target_z):
         for half in (c, 1 - c):
-            remote(w_half(half), own_slot, dev(target_x, target_z, half), when, w_sem(name, c))
-
-    def w_take(name, xo, zo, core):
-        slot = wbuf.at[xo, zo, core]
-        pltpu.make_async_remote_copy(
-            src_ref=slot, dst_ref=slot, send_sem=send_sems.at[0], recv_sem=w_sem(name, core),
-            device_id=sibling, device_id_type=MESH,
-        ).wait_recv()
-        return slot
-
-    w_give(("z", 1), x, z_of[1])
-    w_give(("z", 7), x, z_of[7])
-    w_give(("z", 4), x, z_of[4], c == 1)
-    for d in (1, 3, 2):
-        w_give(("x", d), x_of[d], z)
-    remote(w_half(1 - c), own_slot, sibling, None, w_sem("cross", c))
+            put(w_half(half), own_slot, dev(target_x, target_z, half), kind, (kind, d))
+
+    for d in (4, 1, 7):
+        w_give("z", d, x, z_of[d])
+    for d in (1, 3, 2):
+        w_give("x", d, x_of[d], z)
+    put(w_half(1 - c), own_slot, sibling, "cross", "cross")
     pos_load.wait()
-    pos_copy = remote(pos_ref, pos_sib, sibling)
+    put(pos_ref, pos_sib, sibling, "pos", "pos")
     emb_load.wait()
-    emb_copy = remote(emb_own, emb_sib, sibling)
+    put(emb_own, emb_sib, sibling, "emb", "emb")
     wbuf[x, z, c] = w_ref[:, pl.ds(pl.multiple_of(c * HALF, 128), HALF)]
 
-    def w_send(name, slot, xx, zz, core):
-        remote(slot, slot, dev(xx, zz, c), None, w_sem(name, core))
-
-    def w_along_x(e, slot):
+    onward = {1: ((7, 2),), 7: ((1, 6),), 4: ((1, 3), (7, 5))}
+
+    def w_pass_z(kind, slot, e, name):
+        for to, seen in onward[e]:
+            put(slot, slot, dev(x, z_of[to], c), kind, name(seen))
+
+    def w_along_x(e):
+        piece = wbuf.at[x, z_of[e], 1]
         for d in (1, 3, 2):
-            w_send(("zx", e, d), slot, x_of[d], z, 1)
-
-    def w_ring(way, s, d):
-        if s == 0 and d == 0:
-            return ("z", 1) if way == 0 else ("z", 7)
-        return ("ring", way, s, d)
-
-    def w_ring_step(s):
-        for d in (0, 1, 3, 2):
-            xo = (x - d) % NX
-            for way in (0, 1):
-                if s > (4, 3)[way]:
-                    continue
-                zo = (z - s) % NZ if way == 0 else (z + s) % NZ
-                slot = w_take(w_ring(way, s - 1, d), xo, zo, 0)
-                if s < (4, 3)[way]:
-                    w_send(w_ring(way, s, d), slot, x, z_of[(1, 7)[way]], 0)
+            put(piece, piece, dev(x_of[d], z, c), "bx", ("bx", d))
+
+    def w_from_z(e):
+        slot = take(wbuf.at[x, z_of[e]], ("z", 8 - e))
+        w_pass_z("far", slot, e, lambda seen: ("far", seen))
+        w_along_x(e)
 
     aw_load.wait()
     lane = iota((D, 128), 1)
@@ -163,18 +156,17 @@
     awc[:, 384:512] = pair(6, 8)
     awc[:, 512:640] = pair(4, 7)
 
+    w_from_z(1)
+    w_from_z(7)
     for d in (1, 3, 2):
         xo = (x - d) % NX
-        slot = w_take(("x", d), xo, z, 0)
-        for way in (0, 1):
-            w_send(w_ring(way, 0, d), slot, x, z_of[(1, 7)[way]], 0)
-    for e, onward in ((1, ((7, 2),)), (7, ((1, 6),)), (4, ((1, 3), (7, 5)))):
-        slot = w_take(("z", 8 - e), x, z_of[e], 1)
-        for to, seen in onward:
-            w_send(("far", seen), slot, x, z_of[to], 1)
-        w_along_x(e, slot)
-
-    pos_copy.wait_recv()
+        take(wbuf.at[xo, z], ("x", d))
+        piece = wbuf.at[xo, z, 0]
+        for to in (4, 1, 7):
+            put(piece, piece, dev(x, z_of[to], c), "az", ("az", to, d))
+    w_from_z(4)
+
+    take(pos_sib, "pos")
     pos = jnp.concatenate([pos_ref[...], pos_sib[...]], axis=1)
     slots = 2 * SLOTS
     lane_t = iota((1, slots), 1)
@@ -197,16 +189,19 @@
     marked = jnp.where(row_kind == in_chip, value, 0.0).astype(BF16)
     marks[...] = nt_dot(chip_hot, marked).reshape(NX, 8, 128)
 
-    mark_x = {}
-    for d in (1, 3, 2):
-        mark_x[d] = remote(marks.at[x_of[d]], marks_mid.at[x], dev(x_of[d], z, c))
-
-    w_ring_step(1)
+    for d in (1, 3, 2):
+        put(marks.at[x_of[d]], marks_mid.at[x], dev(x_of[d], z, c), "mark x", "mark x")
+
     for e in (2, 6, 3, 5):
-        w_along_x(e, w_take(("far", e), x, z_of[e], 1))
-
-    for d in (1, 3, 2):
-        mark_x[d].wait_recv()
+        take(wbuf.at[x, z_of[e]], ("far", e))
+        w_along_x(e)
+    for d in (1, 3, 2):
+        xo = (x - d) % NX
+        for e in (1, 7, 4):
+            piece = take(wbuf.at[xo, z_of[e], 0], ("az", 8 - e, d))
+            w_pass_z("afar", piece, e, lambda seen: ("afar", seen))
+
+    take(marks_mid.at[0:3], "mark x")
     lane_group = iota((8, 128), 1) // 32
     merged = jnp.where(lane_group == x, marks[x], 0.0)
     for d in (1, 3, 2):
@@ -214,29 +209,23 @@
         merged = merged + jnp.where(lane_group == xo, marks_mid[xo], 0.0)
     for zz in range(NZ):
         marks_z[zz] = jnp.broadcast_to(merged[zz : zz + 1], (8, 128))
-    mark_z = {}
     for d in range(1, NZ):
-        mark_z[d] = remote(marks_z.at[z_of[d]], marks_got.at[z], dev(x, z_of[d], c))
+        put(marks_z.at[z_of[d]], marks_got.at[z], dev(x, z_of[d], c), "mark z", "mark z")
 
     for d in range(NX):
         rows = iota((256, slots), 0) + x_of[d] * 256
         hot_s[d] = (rows.astype(F32) == target_row).astype(F32).astype(BF16)
 
-    for s in (2, 3, 4):
-        w_ring_step(s)
-    w_take("cross", x, z, 1 - c)
-    for d in (1, 3, 2):
-        w_take(("x", d), (x - d) % NX, z, 1)
-        for e in range(1, NZ):
-            w_take(("zx", e, d), (x - d) % NX, z_of[e], 1)
+    take(wbuf.at[x, z, 1 - c], "cross")
+    for d in (1, 3, 2):
+        take(wbuf.at[(x - d) % NX, 0:7, 1], ("bx", d))
+    for e in (2, 6, 3, 5):
+        take(wbuf.at[0:3, z_of[e], 0], ("afar", e))
 
     weight = wbuf[...].reshape(E, HALF)
     seq[0:SLOTS] = jnp.dot(emb_own[...], weight, preferred_element_type=F32).astype(BF16)
-    emb_copy.wait_recv()
+    take(emb_sib, "emb")
     seq[SLOTS:] = jnp.dot(emb_sib[...], weight, preferred_element_type=F32).astype(BF16)
-
-    out_x = {}
-    z_sent = {}
 
     def rows_for(d):
         rows = jnp.dot(hot_s[d], seq[...], preferred_element_type=F32)
@@ -244,12 +233,12 @@
 
     def send_x(d):
         xout[d - 1] = rows_for(d)
-        out_x[d] = remote(xout.at[d - 1], mid.at[x], dev(x_of[d], z, c))
+        put(xout.at[d - 1], mid.at[x], dev(x_of[d], z, c), "out x", ("out x", d))
 
     def send_z(d):
         xo = (x - d) % NX
         for e in (4, 3, 5, 2, 6, 1, 7):
-            z_sent[d, e] = remote(mid.at[xo, z_of[e]], got.at[z, xo], dev(x, z_of[e], c))
+            put(mid.at[xo, z_of[e]], got.at[z, xo], dev(x, z_of[e], c), "out z", ("out z", e))
 
     send_x(1)
     send_x(3)
@@ -257,7 +246,7 @@
     send_z(0)
     send_x(2)
     for d in (1, 3, 2):
-        out_x[d].wait_recv()
+        take(mid.at[(x - d) % NX], ("out x", d))
         send_z(d)
 
     row = iota((256, 128), 0)
@@ -269,14 +258,13 @@
         return jnp.dot(hot, rows.reshape(128, HALF), preferred_element_type=F32)
 
     total = place(marks_z[z][0:1], mid[:, z])
+    take(marks_got.at[0:7], "mark z")
     for d in (1, 7, 2, 6, 3, 5, 4):
-        mark_z[d].wait_recv()
-        for e in range(NX):
-            z_sent[e, d].wait_recv()
         zo = (z - d) % NZ
+        take(got.at[zo], ("out z", d))
         total = total + place(marks_got[zo][0:1], got[zo])
     seqh[c] = total.astype(BF16)
-    half_copy = remote(seqh.at[c], seqh.at[c], sibling)
+    put(seqh.at[c], seqh.at[c], sibling, "half", "half")
 
     def project(h):
         w = awc[pl.ds(pl.multiple_of(h * HALF, 128), HALF), :]
@@ -286,13 +274,11 @@
         ], axis=0)
 
     part = project(c)
-    half_copy.wait_recv()
+    take(seqh.at[1 - c], "half")
     proj = (part + project(1 - c)).astype(BF16)
     kv[z] = proj[:, 256:640]
 
     in_seg = (z % 4, 3 - z % 4)
-    pair_copies = []
-    flow = {}
 
     def low_sent(i, s):
         return None if s < 3 else (i == 3) | (i == 0)
@@ -309,27 +295,28 @@
     def origin(way, s):
         return (z - s) % NZ if way == 0 else (z + s) % NZ
 
+    def piece_of(way, part, s, k):
+        return kv.at[origin(way, s), pl.ds(k * 64 + (0 if part == "low" else 128), 64)]
+
     def pass_on(way, part, s, k):
-        sent = low_sent if part == "low" else rest_sent
-        block = kv.at[origin(way, s), pl.ds(k * 64 + (0 if part == "low" else 128), 64)]
-        flow[way, part, s, k] = remote(block, block, (right, left)[way], sent(in_seg[way], s))
-
-    def wait_for(copy, when):
-        if when is None:
-            copy.wait_recv()
-        else:
-            pl.when(when)(copy.wait_recv)
-
-    def to_pair(zo, when=None):
+        when = low_sent(in_seg[way], s) if part == "low" else rest_sent(in_seg[way], s)
+        block = piece_of(way, part, s, k)
+        kind = (way, "low") if part == "low" and s < 3 else (way, part, s)
+        put(block, block, (right, left)[way], kind, (way, part, s, k), when)
+
+    def take_piece(way, part, s, k):
+        when = low_got(in_seg[way], s) if part == "low" else rest_got(in_seg[way], s)
+        take(piece_of(way, part, s + 1, k), (way, part, s, k), when)
+
+    def to_pair(zo, group, when=None):
         for rows, cols in ((0, slice(0, 256)), (64, slice(256, 384))):
-            copy = remote(kv.at[zo, rows : rows + 64, cols], c2.at[zo, :, cols], x_pair, when)
-            pair_copies.append((copy, when))
+            put(kv.at[zo, rows : rows + 64, cols], c2.at[zo, :, cols], x_pair, group, group, when)
 
     for part in ("low", "rest"):
         for k in (0, 1):
             for way in (0, 1):
                 pass_on(way, part, 0, k)
-    to_pair(z)
+    to_pair(z, "pair 0")
 
     lane256 = iota((256, 128), 1)
     q01 = proj[:, 0:128].astype(F32)
@@ -384,9 +371,8 @@
                 mask_s[h // 2, 0:128, 0:128] - 1.0,
             )
 
-    def pair_block(copies, offsets):
-        for copy, when in copies:
-            wait_for(copy, when)
+    def pair_block(group, offsets):
+        take(c2.at[0 : len(offsets)], group)
         blocks = [c2[z_of[e]] for e in offsets]
         block = jnp.concatenate(blocks, axis=0)
         for h in range(3):
@@ -399,19 +385,19 @@
     for s in range(4):
         for k in (0, 1):
             for way in (0, 1):
-                wait_for(flow[way, "low", s, k], low_got(in_seg[way], s))
+                take_piece(way, "low", s, k)
                 if s < 3:
                     pass_on(way, "low", s + 1, k)
         for way in (0, 1):
-            to_pair(origin(way, s + 1), low_got(in_seg[way], s))
+            to_pair(origin(way, s + 1), "pair 0" if s < 2 else "pair 1", low_got(in_seg[way], s))
         if s < 3:
             for k in (0, 1):
                 for way in (0, 1):
-                    pl.when(rest_got(in_seg[way], s))(flow[way, "rest", s, k].wait_recv)
+                    take_piece(way, "rest", s, k)
                     if s < 2:
                         pass_on(way, "rest", s + 1, k)
         if s == 3:
-            pair_block(pair_copies[:10], (0, 7, 1, 6, 2))
+            pair_block("pair 0", (0, 7, 1, 6, 2))
         for way in (0, 1):
             zo = origin(way, s + 1)
             got_low = low_got(in_seg[way], s)
@@ -422,7 +408,7 @@
                 pl.when(part if got_low is None else part & got_low)(lambda: part_block(zo))
             else:
                 pl.when(got_low)(lambda: part_block(zo))
-    pair_block(pair_copies[10:], (3, 5, 4))
+    pair_block("pair 1", (3, 5, 4))
 
     heads = [acc_s[h] / l_s[h] for h in range(3)]
     done = jnp.concatenate(
@@ -444,17 +430,27 @@
         ], axis=1)
 
     fin[0] = arranged(1 - c).astype(BF16)
-    fin_copy = remote(fin.at[0], fin.at[1], sibling)
+    put(fin.at[0], fin.at[1], sibling, "fin", "fin")
     mine = arranged(c)
-    fin_copy.wait_recv()
+    take(fin.at[1], "fin")
     own_lane = (iota((128, HALF), 1) // 64) % 2 == c
     out_ref[...] = jnp.where(own_lane, mine, fin[1].astype(F32)).astype(BF16)
 
-    for copy, when in started:
-        if when is None:
-            copy.wait_send()
-        else:
-            pl.when(when)(copy.wait_send)
+    for kind, ref in (
+        ("z", wbuf.at[0, 0:3]), ("x", wbuf.at[0, 0:3]), ("cross", wbuf.at[0, 0, 0]), ("far", wbuf.at[0, 0:4]),
+        ("bx", wbuf.at[0:3, 0:7, 0]), ("az", wbuf.at[0:3, 0:3, 0]), ("afar", wbuf.at[0:3, 0:4, 0]),
+        ("pos", pos_sib), ("emb", emb_sib), ("mark x", marks_mid.at[0:3]), ("mark z", marks_got.at[0:7]),
+        ("out x", xout), ("out z", got.at[0:7]), ("half", seqh.at[0]), ("fin", fin.at[0]),
+        ("pair 0", c2.at[0:5]), ("pair 1", c2.at[0:3]),
+    ):
+        sent(ref, kind)
+    for way in (0, 1):
+        i = in_seg[way]
+        sent(kv.at[0:3, 0:128], (way, "low"))
+        sent(kv.at[0, 0:128], (way, "low", 3), low_sent(i, 3))
+        for s in (0, 1, 2):
+            sent(kv.at[0, 0:128], (way, "rest", s), rest_sent(i, s))
+    assert len(names) <= N_SEMS, len(names)
 
 
 def local(tile_embeddings, tile_position, input_weight, attention_weight):
@@ -487,9 +483,7 @@
         pltpu.VMEM((2, 256, 256), F32),
         pltpu.VMEM((2, 128, HALF), BF16),
         pltpu.VMEM((2, 256, HALF), BF16),
-        pltpu.SemaphoreType.DMA((N_COPIES,)),
-        pltpu.SemaphoreType.DMA((N_COPIES,)),
-        pltpu.SemaphoreType.DMA((2 * N_W,)),
+        pltpu.SemaphoreType.DMA((N_SEMS,)),
         pltpu.SemaphoreType.DMA((4,)),
     ]
     return pl.pallas_call(

time: 83.7 us -> 79.3 us (0.947)
  Pallas kernels: 82 us -> 77.6 us
    pallas_call x1, Pallas kernels: 82 us -> 77.6 us  [local(): pl.pallas_call(kernel, out_shape=jax.ShapeDtypeStruct((TOK_DEV, HALF), BF...]
where the time goes in v3:
time: 79.3 us; the launch traced here: 79.1 us
  Pallas kernels  77.6 us (98%)
  local copies, waits for them, and re-layouts  1.54 us (2%)
    pallas_call x1, Pallas kernels, local(): pl.pallas_call(kernel, out_shape=jax.ShapeDtypeStruct((TOK_DEV, HALF), BF...  77.6 us

profile of v3, /device:TPU:1, one launch (start us, length us, event | category | flops | bytes accessed | tf_op | source)
XLA Modules:
  0.0 79.1 jit_solution(8437048269423339560)
XLA Ops:
  0.0 77.6 %shard_map.46 = bf16[128,384]{1,0:T(8,128)(2,1)} custom-call(bf16[256,1536]{1,0:T(8,128)(2,1)} %emb_in.1, s32[1,256]{1,0:T(1,128)} %bitcast.1, bf16[24,768]{1,0:T(8,128)(2,1)} %w_in.1, bf16[768,1152]{1,0:T(8,128)(2,1)} %aw_in.1), custom_call_target="tpu_custom_call" | custom-call | tf_op jit(solution)/shard_map/pallas_call | solution.py:489
  77.6 1.5 %copy.6 = bf16[128,384]{1,0:T(8,128)(2,1)} copy(bf16[128,384]{1,0:T(8,128)(2,1)} %shard_map.46) | data formatting | bytes 196608

commit v4 on v3

--- a/solution.py
+++ b/solution.py
@@ -33,7 +33,7 @@
     return jnp.concatenate([a[:, 64:], a[:, :64]], axis=1)
 
 
-N_SEMS = 100
+N_SEMS = 112
 
 
 def kernel(
@@ -41,7 +41,7 @@
     pos_ref, w_ref,
     emb_own, emb_sib, pos_sib, wbuf, awbuf, awc,
     marks, marks_mid, marks_z, marks_got,
-    hot_s, seq, mid, got, xout, kv, c2, qm, m_s, l_s, acc_s, mask_s, fin, seqh,
+    hot_s, seq, mid, got, xout, kv, c2, qm, m_s, l_s, acc_s, mask_s, low_mask_s, fin, seqh,
     sems, local_sems,
 ):
     me = lax.axis_index("seq")
@@ -139,32 +139,6 @@
         slot = take(wbuf.at[x, z_of[e]], ("z", 8 - e))
         w_pass_z("far", slot, e, lambda seen: ("far", seen))
         w_along_x(e)
-
-    aw_load.wait()
-    lane = iota((D, 128), 1)
-
-    def pair(group_a, group_b):
-        a = awbuf[:, group_a * 128 : group_a * 128 + 128].astype(F32)
-        b = awbuf[:, group_b * 128 : group_b * 128 + 128].astype(F32)
-        even = jnp.where(lane < 64, a, roll64(b))
-        odd = jnp.where(lane < 64, roll64(a), b)
-        return jnp.where(c == 0, even, odd).astype(BF16)
-
-    awc[:, 0:128] = pair(0, 2)
-    awc[:, 128:256] = pair(1, 1)
-    awc[:, 256:384] = pair(3, 5)
-    awc[:, 384:512] = pair(6, 8)
-    awc[:, 512:640] = pair(4, 7)
-
-    w_from_z(1)
-    w_from_z(7)
-    for d in (1, 3, 2):
-        xo = (x - d) % NX
-        take(wbuf.at[xo, z], ("x", d))
-        piece = wbuf.at[xo, z, 0]
-        for to in (4, 1, 7):
-            put(piece, piece, dev(x, z_of[to], c), "az", ("az", to, d))
-    w_from_z(4)
 
     take(pos_sib, "pos")
     pos = jnp.concatenate([pos_ref[...], pos_sib[...]], axis=1)
@@ -185,12 +159,27 @@
     in_chip = jnp.where(pos >= 0, ((owner % 2) * 16 + source_core * 8).astype(F32) + rank, -1.0)
     chip_hot = (iota((32, slots), 0) == chip).astype(F32).astype(BF16)
     value = ((pos & 255) + 1).astype(F32)
-    row_kind = (iota((128, slots), 0) % 32).astype(F32)
+    kind = iota((128, slots), 0)
+    row_kind = (kind // 64 * 16 + kind % 16).astype(F32)
     marked = jnp.where(row_kind == in_chip, value, 0.0).astype(BF16)
     marks[...] = nt_dot(chip_hot, marked).reshape(NX, 8, 128)
 
     for d in (1, 3, 2):
         put(marks.at[x_of[d]], marks_mid.at[x], dev(x_of[d], z, c), "mark x", "mark x")
+
+    for d in range(NX):
+        rows = iota((256, slots), 0) + x_of[d] * 256
+        hot_s[d] = (rows.astype(F32) == target_row).astype(F32).astype(BF16)
+
+    w_from_z(1)
+    w_from_z(7)
+    for d in (1, 3, 2):
+        xo = (x - d) % NX
+        take(wbuf.at[xo, z], ("x", d))
+        piece = wbuf.at[xo, z, 0]
+        for to in (4, 1, 7):
+            put(piece, piece, dev(x, z_of[to], c), "az", ("az", to, d))
+    w_from_z(4)
 
     for e in (2, 6, 3, 5):
         take(wbuf.at[x, z_of[e]], ("far", e))
@@ -202,7 +191,7 @@
             w_pass_z("afar", piece, e, lambda seen: ("afar", seen))
 
     take(marks_mid.at[0:3], "mark x")
-    lane_group = iota((8, 128), 1) // 32
+    lane_group = iota((8, 128), 1) % 64 // 16
     merged = jnp.where(lane_group == x, marks[x], 0.0)
     for d in (1, 3, 2):
         xo = (x - d) % NX
@@ -212,10 +201,6 @@
     for d in range(1, NZ):
         put(marks_z.at[z_of[d]], marks_got.at[z], dev(x, z_of[d], c), "mark z", "mark z")
 
-    for d in range(NX):
-        rows = iota((256, slots), 0) + x_of[d] * 256
-        hot_s[d] = (rows.astype(F32) == target_row).astype(F32).astype(BF16)
-
     take(wbuf.at[x, z, 1 - c], "cross")
     for d in (1, 3, 2):
         take(wbuf.at[(x - d) % NX, 0:7, 1], ("bx", d))
@@ -229,54 +214,79 @@
 
     def rows_for(d):
         rows = jnp.dot(hot_s[d], seq[...], preferred_element_type=F32)
-        return rows.astype(BF16).reshape(NZ, 32, HALF)
-
-    def send_x(d):
-        xout[d - 1] = rows_for(d)
-        put(xout.at[d - 1], mid.at[x], dev(x_of[d], z, c), "out x", ("out x", d))
-
-    def send_z(d):
+        return rows.astype(BF16).reshape(NZ, 2, 16, HALF)
+
+    def send_x(d, oc):
+        put(xout.at[d - 1, :, oc], mid.at[x, :, oc], dev(x_of[d], z, c), "out x", ("out x", d, oc))
+
+    def send_z(d, oc):
         xo = (x - d) % NX
         for e in (4, 3, 5, 2, 6, 1, 7):
-            put(mid.at[xo, z_of[e]], got.at[z, xo], dev(x, z_of[e], c), "out z", ("out z", e))
-
-    send_x(1)
-    send_x(3)
+            put(mid.at[xo, z_of[e], oc], got.at[z, oc, xo], dev(x, z_of[e], c), "out z", ("out z", e, oc))
+
+    for d in (1, 3):
+        xout[d - 1] = rows_for(d)
+        send_x(d, 0)
     mid[x] = rows_for(0)
-    send_z(0)
-    send_x(2)
-    for d in (1, 3, 2):
-        take(mid.at[(x - d) % NX], ("out x", d))
-        send_z(d)
-
-    row = iota((256, 128), 0)
-    group = row // 64
-    wanted = (((row % 64) // 32) * 128 + (row % 32) * 4 + (group % 2) * 2 + group // 2 + 1).astype(F32)
-
-    def place(zo_marks, rows):
-        hot = (zo_marks == wanted).astype(F32).astype(BF16)
-        return jnp.dot(hot, rows.reshape(128, HALF), preferred_element_type=F32)
-
-    total = place(marks_z[z][0:1], mid[:, z])
+    send_z(0, 0)
+    xout[1] = rows_for(2)
+    send_x(2, 0)
+    for d in (1, 3, 2):
+        send_x(d, 1)
+    send_z(0, 1)
+    for oc in (0, 1):
+        for d in (1, 3, 2):
+            take(mid.at[(x - d) % NX, :, oc], ("out x", d, oc))
+            send_z(d, oc)
+
+    aw_load.wait()
+    lane = iota((D, 128), 1)
+
+    def pair(group_a, group_b):
+        a = awbuf[:, group_a * 128 : group_a * 128 + 128].astype(F32)
+        b = awbuf[:, group_b * 128 : group_b * 128 + 128].astype(F32)
+        even = jnp.where(lane < 64, a, roll64(b))
+        odd = jnp.where(lane < 64, roll64(a), b)
+        return jnp.where(c == 0, even, odd).astype(BF16)
+
+    awc[:, 0:128] = pair(0, 2)
+    awc[:, 128:256] = pair(1, 1)
+    awc[:, 256:384] = pair(3, 5)
+    awc[:, 384:512] = pair(6, 8)
+    awc[:, 512:640] = pair(4, 7)
+
+    row = iota((128, 64), 0)
+    group = row // 32
+    first_wanted = row % 32 * 4 + group % 2 * 2 + group // 2 + 1
+
+    def place(oc, zo_marks, rows):
+        wanted = (first_wanted + oc * 128).astype(F32)
+        hot = (zo_marks[:, oc * 64 : oc * 64 + 64] == wanted).astype(F32).astype(BF16)
+        return jnp.dot(hot, rows.reshape(64, HALF), preferred_element_type=F32)
+
+    def project(h, oc):
+        w = awc[pl.ds(pl.multiple_of(h * HALF, 128), HALF), :]
+        rows = jnp.concatenate([
+            seqh[h, oc, pl.ds(pl.multiple_of(c * 64, 64), 64), :],
+            seqh[h, oc, pl.ds(pl.multiple_of((1 - c) * 64, 64), 64), :],
+        ], axis=0)
+        return jnp.dot(rows, w, preferred_element_type=F32)
+
     take(marks_got.at[0:7], "mark z")
-    for d in (1, 7, 2, 6, 3, 5, 4):
-        zo = (z - d) % NZ
-        take(got.at[zo], ("out z", d))
-        total = total + place(marks_got[zo][0:1], got[zo])
-    seqh[c] = total.astype(BF16)
-    put(seqh.at[c], seqh.at[c], sibling, "half", "half")
-
-    def project(h):
-        w = awc[pl.ds(pl.multiple_of(h * HALF, 128), HALF), :]
-        return jnp.concatenate([
-            jnp.dot(seqh[h, pl.ds(pl.multiple_of(c * 128, 128), 128), :], w, preferred_element_type=F32),
-            jnp.dot(seqh[h, pl.ds(pl.multiple_of((1 - c) * 128, 128), 128), :], w, preferred_element_type=F32),
-        ], axis=0)
-
-    part = project(c)
-    take(seqh.at[1 - c], "half")
-    proj = (part + project(1 - c)).astype(BF16)
-    kv[z] = proj[:, 256:640]
+
+    def projections_of(oc):
+        total = place(oc, marks_z[z][0:1], mid[:, z, oc])
+        for d in (1, 7, 2, 6, 3, 5, 4):
+            zo = (z - d) % NZ
+            take(got.at[zo, oc], ("out z", d, oc))
+            total = total + place(oc, marks_got[zo][0:1], got[zo, oc])
+        seqh[c, oc] = total.astype(BF16)
+        put(seqh.at[c, oc], seqh.at[c, oc], sibling, "half", ("half", oc))
+        part = project(c, oc)
+        take(seqh.at[1 - c, oc], ("half", oc))
+        proj = (part + project(1 - c, oc)).astype(BF16)
+        kv[z, oc] = proj[:, 256:640]
+        return proj
 
     in_seg = (z % 4, 3 - z % 4)
 
@@ -296,7 +306,7 @@
         return (z - s) % NZ if way == 0 else (z + s) % NZ
 
     def piece_of(way, part, s, k):
-        return kv.at[origin(way, s), pl.ds(k * 64 + (0 if part == "low" else 128), 64)]
+        return kv.at[origin(way, s), k, pl.ds(0 if part == "low" else 64, 64)]
 
     def pass_on(way, part, s, k):
         when = low_sent(in_seg[way], s) if part == "low" else rest_sent(in_seg[way], s)
@@ -308,27 +318,38 @@
         when = low_got(in_seg[way], s) if part == "low" else rest_got(in_seg[way], s)
         take(piece_of(way, part, s + 1, k), (way, part, s, k), when)
 
-    def to_pair(zo, group, when=None):
-        for rows, cols in ((0, slice(0, 256)), (64, slice(256, 384))):
-            put(kv.at[zo, rows : rows + 64, cols], c2.at[zo, :, cols], x_pair, group, group, when)
-
-    for part in ("low", "rest"):
-        for k in (0, 1):
+    def to_pair(zo, oc, group, when=None):
+        for rows, cols in ((0, slice(0, 256)), (32, slice(256, 384))):
+            put(
+                kv.at[zo, oc, rows : rows + 32, cols], c2.at[zo, oc * 32 : oc * 32 + 32, cols], x_pair,
+                group, group, when,
+            )
+
+    projected = []
+    for oc in (0, 1):
+        projected.append(projections_of(oc).astype(F32))
+        for part in ("low", "rest"):
             for way in (0, 1):
-                pass_on(way, part, 0, k)
-    to_pair(z, "pair 0")
+                pass_on(way, part, 0, oc)
+        to_pair(z, oc, "pair 0")
 
     lane256 = iota((256, 128), 1)
-    q01 = proj[:, 0:128].astype(F32)
-    q2 = proj[:, 128:256].astype(F32)
+    query = jnp.concatenate(
+        [projected[oc][g * 32 : g * 32 + 32, 0:256] for g in range(4) for oc in (0, 1)], axis=0
+    )
+    q01 = query[:, 0:128]
+    q2 = query[:, 128:256]
     qm[0] = jnp.where(lane256 < 64, q01, 0.0).astype(BF16)
     qm[1] = jnp.where(lane256 < 64, 0.0, q01).astype(BF16)
     qm[2] = jnp.where(lane256 < 64, q2, 0.0).astype(BF16)
 
-    rr, cc = iota((256, 256), 0), iota((256, 256), 1)
-    both = jnp.where((rr < 128) & (cc < 128), 2.0, 1.0)
-    mask_s[0] = both + jnp.where((rr < 64) & (cc < 64), 1.0, 0.0)
-    mask_s[1] = both + jnp.where((rr >= 64) & (rr < 128) & (cc >= 64) & (cc < 128), 1.0, 0.0)
+    rr, cc = iota((128, 256), 0), iota((128, 256), 1) % 128
+    low_col = jnp.where(cc < 64, 2.0, 1.0)
+    mask_s[0] = low_col + jnp.where((rr < 64) & (cc < 32), 1.0, 0.0)
+    mask_s[1] = low_col + jnp.where((rr >= 64) & (cc >= 32) & (cc < 64), 1.0, 0.0)
+    low_mask = [jnp.concatenate([mask_s[n, :, 0:64], mask_s[n, :, 128:192]], axis=1) - 1.0 for n in (0, 1)]
+    for n in (0, 1):
+        low_mask_s[n] = low_mask[n]
 
     key_cols = (0, 0, 256)
     value_cols = (128, 128, 256)
@@ -344,7 +365,9 @@
             m_new = jnp.maximum(m_old, top)
             keep = jnp.exp2((m_old - m_new) * EXP2_SCALE)
         p = jnp.exp2((s - m_new) * EXP2_SCALE)
-        if mult is not None:
+        if rows == 256:
+            p = jnp.concatenate([p[0:128] * mult, p[128:]], axis=0)
+        elif mult is not None:
             p = p * mult
         total_p = jnp.sum(p, axis=1, keepdims=True)
         pv = jnp.dot(p.astype(BF16), values, preferred_element_type=F32)
@@ -356,59 +379,75 @@
             l_s[h, at, :] = l_s[h, at, :] * keep + total_p
             acc_s[h, at, :] = acc_s[h, at, :] * keep + pv
 
-    def full_block(zo, fresh=False):
-        for h in range(3):
-            update(
-                h, 0, 256, kv[zo, :, key_cols[h] : key_cols[h] + 128],
-                kv[zo, :, value_cols[h] : value_cols[h] + 128], mask_s[h // 2], fresh,
-            )
-
-    def part_block(zo):
-        for h in range(3):
-            update(
-                h, 0, 128, kv[zo, 0:128, key_cols[h] : key_cols[h] + 128],
-                kv[zo, 0:128, value_cols[h] : value_cols[h] + 128],
-                mask_s[h // 2, 0:128, 0:128] - 1.0,
-            )
-
-    def pair_block(group, offsets):
-        take(c2.at[0 : len(offsets)], group)
-        blocks = [c2[z_of[e]] for e in offsets]
-        block = jnp.concatenate(blocks, axis=0)
-        for h in range(3):
-            update(
-                h, 64 * (h // 2), 64, block[:, key_cols[h] : key_cols[h] + 128],
-                block[:, value_cols[h] : value_cols[h] + 128], None,
-            )
-
-    full_block(z, fresh=True)
+    def full_head(zo, h, fresh=False):
+        update(
+            h, 0, 256, kv[zo, :, :, key_cols[h] : key_cols[h] + 128].reshape(256, 128),
+            kv[zo, :, :, value_cols[h] : value_cols[h] + 128].reshape(256, 128), mask_s[h // 2], fresh,
+        )
+
+    def part_head(zo, h):
+        update(
+            h, 0, 128, kv[zo, :, 0:64, key_cols[h] : key_cols[h] + 128].reshape(128, 128),
+            kv[zo, :, 0:64, value_cols[h] : value_cols[h] + 128].reshape(128, 128), low_mask_s[h // 2],
+        )
+
+    def pair_head(offsets, h):
+        at = lambda e, col: c2[z_of[e], :, col : col + 128]
+        update(
+            h, 64 * (h // 2), 64, jnp.concatenate([at(e, key_cols[h]) for e in offsets], axis=0),
+            jnp.concatenate([at(e, value_cols[h]) for e in offsets], axis=0), None,
+        )
+
+    tasks = []
+
+    def run(count):
+        for _ in range(min(count, len(tasks))):
+            tasks.pop(0)()
+
+    def arrived_head(way, s, h):
+        zo = origin(way, s + 1)
+        if s == 3:
+            pl.when(low_got(in_seg[way], s))(lambda: part_head(zo, h))
+        else:
+            full = rest_got(in_seg[way], s)
+            pl.when(full)(lambda: full_head(zo, h))
+            pl.when(jnp.logical_not(full))(lambda: part_head(zo, h))
+
+    def later(action, *args):
+        tasks.append(lambda: action(*args))
+
+    for h in range(3):
+        full_head(z, h, fresh=True)
     for s in range(4):
         for k in (0, 1):
+            run(1)
             for way in (0, 1):
                 take_piece(way, "low", s, k)
                 if s < 3:
                     pass_on(way, "low", s + 1, k)
-        for way in (0, 1):
-            to_pair(origin(way, s + 1), "pair 0" if s < 2 else "pair 1", low_got(in_seg[way], s))
+                to_pair(
+                    origin(way, s + 1), k, "pair 0" if s < 2 else "pair 1",
+                    None if s < 3 else low_got(in_seg[way], s),
+                )
         if s < 3:
             for k in (0, 1):
+                run(2)
                 for way in (0, 1):
                     take_piece(way, "rest", s, k)
                     if s < 2:
                         pass_on(way, "rest", s + 1, k)
-        if s == 3:
-            pair_block("pair 0", (0, 7, 1, 6, 2))
         for way in (0, 1):
-            zo = origin(way, s + 1)
-            got_low = low_got(in_seg[way], s)
-            if s < 3:
-                full = rest_got(in_seg[way], s)
-                pl.when(full)(lambda: full_block(zo))
-                part = jnp.logical_not(full)
-                pl.when(part if got_low is None else part & got_low)(lambda: part_block(zo))
-            else:
-                pl.when(got_low)(lambda: part_block(zo))
-    pair_block("pair 1", (3, 5, 4))
+            for h in range(3):
+                later(arrived_head, way, s, h)
+        if s == 2:
+            run(3)
+            take(c2.at[0:5], "pair 0")
+            for h in range(3):
+                later(pair_head, (0, 7, 1, 6, 2), h)
+    run(len(tasks))
+    take(c2.at[0:3], "pair 1")
+    for h in range(3):
+        pair_head((3, 5, 4), h)
 
     heads = [acc_s[h] / l_s[h] for h in range(3)]
     done = jnp.concatenate(
@@ -446,10 +485,10 @@
         sent(ref, kind)
     for way in (0, 1):
         i = in_seg[way]
-        sent(kv.at[0:3, 0:128], (way, "low"))
-        sent(kv.at[0, 0:128], (way, "low", 3), low_sent(i, 3))
+        sent(kv.at[0:3, :, 0:64], (way, "low"))
+        sent(kv.at[0, :, 0:64], (way, "low", 3), low_sent(i, 3))
         for s in (0, 1, 2):
-            sent(kv.at[0, 0:128], (way, "rest", s), rest_sent(i, s))
+            sent(kv.at[0, :, 0:64], (way, "rest", s), rest_sent(i, s))
     assert len(names) <= N_SEMS, len(names)
 
 
@@ -471,18 +510,19 @@
         pltpu.VMEM((NZ, 8, 128), F32),
         pltpu.VMEM((NX, 256, 2 * SLOTS), BF16),
         pltpu.VMEM((2 * SLOTS, HALF), BF16),
-        pltpu.VMEM((NX, NZ, 32, HALF), BF16),
-        pltpu.VMEM((NZ, NX, 32, HALF), BF16),
-        pltpu.VMEM((3, NZ, 32, HALF), BF16),
-        pltpu.VMEM((NZ, 256, HALF), BF16),
+        pltpu.VMEM((NX, NZ, 2, 16, HALF), BF16),
+        pltpu.VMEM((NZ, 2, NX, 16, HALF), BF16),
+        pltpu.VMEM((3, NZ, 2, 16, HALF), BF16),
+        pltpu.VMEM((NZ, 2, 128, HALF), BF16),
         pltpu.VMEM((NZ, 64, HALF), BF16),
         pltpu.VMEM((3, 256, 128), BF16),
         pltpu.VMEM((3, 256, 1), F32),
         pltpu.VMEM((3, 256, 1), F32),
         pltpu.VMEM((3, 256, 128), F32),
-        pltpu.VMEM((2, 256, 256), F32),
+        pltpu.VMEM((2, 128, 256), F32),
+        pltpu.VMEM((2, 128, 128), F32),
         pltpu.VMEM((2, 128, HALF), BF16),
-        pltpu.VMEM((2, 256, HALF), BF16),
+        pltpu.VMEM((2, 2, 128, HALF), BF16),
         pltpu.SemaphoreType.DMA((N_SEMS,)),
         pltpu.SemaphoreType.DMA((4,)),
     ]

time: 79.3 us -> 76.6 us (0.966)
  Pallas kernels: 77.6 us -> 74.9 us
    pallas_call x1, Pallas kernels: 77.6 us -> 74.9 us  [local(): pl.pallas_call(kernel, out_shape=jax.ShapeDtypeStruct((TOK_DEV, HALF), BF...]
where the time goes in v4:
time: 76.6 us; the launch traced here: 76.5 us
  Pallas kernels  74.9 us (98%)
  local copies, waits for them, and re-layouts  1.54 us (2%)
    pallas_call x1, Pallas kernels, local(): pl.pallas_call(kernel, out_shape=jax.ShapeDtypeStruct((TOK_DEV, HALF), BF...  74.9 us
    unnamed x1, local copies, waits for them, and re-layouts  1.54 us

profile of v4, /device:TPU:1, one launch (start us, length us, event | category | flops | bytes accessed | tf_op | source)
XLA Modules:
  0.0 76.5 jit_solution(15989564301854940787)
XLA Ops:
  0.0 74.9 %shard_map.46 = bf16[128,384]{1,0:T(8,128)(2,1)} custom-call(bf16[256,1536]{1,0:T(8,128)(2,1)} %emb_in.1, s32[1,256]{1,0:T(1,128)} %bitcast.1, bf16[24,768]{1,0:T(8,128)(2,1)} %w_in.1, bf16[768,1152]{1,0:T(8,128)(2,1)} %aw_in.1), custom_call_target="tpu_custom_call" | custom-call | tf_op jit(solution)/shard_map/pallas_call | solution.py:529
  74.9 1.5 %copy.6 = bf16[128,384]{1,0:T(8,128)(2,1)} copy(bf16[128,384]{1,0:T(8,128)(2,1)} %shard_map.46) | data formatting | bytes 196608

commit v5 on v4

--- a/solution.py
+++ b/solution.py
@@ -33,7 +33,7 @@
     return jnp.concatenate([a[:, 64:], a[:, :64]], axis=1)
 
 
-N_SEMS = 112
+N_SEMS = 113
 
 
 def kernel(
@@ -97,7 +97,7 @@
 
     barrier = pltpu.get_barrier_semaphore()
     partners = [sibling] + [dev(x_of[d], z, c) for d in (1, 2, 3)] + [dev(x, z_of[d], c) for d in range(1, 8)]
-    partners += [dev(x_of[d], z, 1 - c) for d in (1, 2, 3)] + [dev(x, z_of[d], 1 - c) for d in (1, 4, 7)]
+    partners += [dev(x_of[d], z, 1 - c) for d in (1, 2, 3)] + [dev(x, z_of[d], 1 - c) for d in (1, 2, 6, 7)]
     for partner in partners:
         pl.semaphore_signal(barrier, inc=1, device_id=partner, device_id_type=MESH)
     pl.semaphore_wait(barrier, len(partners))
@@ -113,7 +113,7 @@
         for half in (c, 1 - c):
             put(w_half(half), own_slot, dev(target_x, target_z, half), kind, (kind, d))
 
-    for d in (4, 1, 7):
+    for d in (2, 6, 1, 7):
         w_give("z", d, x, z_of[d])
     for d in (1, 3, 2):
         w_give("x", d, x_of[d], z)
@@ -124,21 +124,13 @@
     put(emb_own, emb_sib, sibling, "emb", "emb")
     wbuf[x, z, c] = w_ref[:, pl.ds(pl.multiple_of(c * HALF, 128), HALF)]
 
-    onward = {1: ((7, 2),), 7: ((1, 6),), 4: ((1, 3), (7, 5))}
-
-    def w_pass_z(kind, slot, e, name):
-        for to, seen in onward[e]:
-            put(slot, slot, dev(x, z_of[to], c), kind, name(seen))
+    def w_to(kind, piece, to, name):
+        put(piece, piece, dev(x, z_of[to], c), kind, name)
 
     def w_along_x(e):
         piece = wbuf.at[x, z_of[e], 1]
         for d in (1, 3, 2):
             put(piece, piece, dev(x_of[d], z, c), "bx", ("bx", d))
-
-    def w_from_z(e):
-        slot = take(wbuf.at[x, z_of[e]], ("z", 8 - e))
-        w_pass_z("far", slot, e, lambda seen: ("far", seen))
-        w_along_x(e)
 
     take(pos_sib, "pos")
     pos = jnp.concatenate([pos_ref[...], pos_sib[...]], axis=1)
@@ -171,24 +163,38 @@
         rows = iota((256, slots), 0) + x_of[d] * 256
         hot_s[d] = (rows.astype(F32) == target_row).astype(F32).astype(BF16)
 
-    w_from_z(1)
-    w_from_z(7)
+    def w_from_x(d):
+        take(wbuf.at[(x - d) % NX, z], ("x", d))
+        piece = wbuf.at[(x - d) % NX, z, 0]
+        for to in (2, 6, 1, 7):
+            w_to("az", piece, to, ("az", to, d))
+
+    w_from_x(1)
+    w_from_x(3)
+    for e, core, to, seen in ((2, 0, 7, 3), (6, 1, 1, 5)):
+        block = take(wbuf.at[x, z_of[e]], ("z", 8 - e))
+        w_to("far", block, to, ("far", seen))
+        w_to("far", wbuf.at[x, z_of[e], core], 8 - e, ("far", 4))
+    w_from_x(2)
+    for e in (1, 7):
+        take(wbuf.at[x, z_of[e]], ("z", 8 - e))
+    for e in (2, 6, 1, 7):
+        w_along_x(e)
+
     for d in (1, 3, 2):
         xo = (x - d) % NX
-        take(wbuf.at[xo, z], ("x", d))
-        piece = wbuf.at[xo, z, 0]
-        for to in (4, 1, 7):
-            put(piece, piece, dev(x, z_of[to], c), "az", ("az", to, d))
-    w_from_z(4)
-
-    for e in (2, 6, 3, 5):
-        take(wbuf.at[x, z_of[e]], ("far", e))
-        w_along_x(e)
-    for d in (1, 3, 2):
-        xo = (x - d) % NX
-        for e in (1, 7, 4):
+        for e, to, seen in ((2, 7, 3), (6, 1, 5)):
             piece = take(wbuf.at[xo, z_of[e], 0], ("az", 8 - e, d))
-            w_pass_z("afar", piece, e, lambda seen: ("afar", seen))
+            w_to("afar", piece, to, ("afar", seen))
+            if (e == 2) == (d != 3):
+                w_to("afar", piece, 8 - e, ("afar", 4))
+        if d == 3:
+            for e in (3, 5, 4):
+                take(wbuf.at[x, z_of[e]], ("far", e))
+                w_along_x(e)
+    for d in (1, 3, 2):
+        for e in (1, 7):
+            take(wbuf.at[(x - d) % NX, z_of[e], 0], ("az", 8 - e, d))
 
     take(marks_mid.at[0:3], "mark x")
     lane_group = iota((8, 128), 1) % 64 // 16
@@ -204,7 +210,7 @@
     take(wbuf.at[x, z, 1 - c], "cross")
     for d in (1, 3, 2):
         take(wbuf.at[(x - d) % NX, 0:7, 1], ("bx", d))
-    for e in (2, 6, 3, 5):
+    for e in (3, 5, 4):
         take(wbuf.at[0:3, z_of[e], 0], ("afar", e))
 
     weight = wbuf[...].reshape(E, HALF)
@@ -476,8 +482,8 @@
     out_ref[...] = jnp.where(own_lane, mine, fin[1].astype(F32)).astype(BF16)
 
     for kind, ref in (
-        ("z", wbuf.at[0, 0:3]), ("x", wbuf.at[0, 0:3]), ("cross", wbuf.at[0, 0, 0]), ("far", wbuf.at[0, 0:4]),
-        ("bx", wbuf.at[0:3, 0:7, 0]), ("az", wbuf.at[0:3, 0:3, 0]), ("afar", wbuf.at[0:3, 0:4, 0]),
+        ("z", wbuf.at[0, 0:4]), ("x", wbuf.at[0, 0:3]), ("cross", wbuf.at[0, 0, 0]), ("far", wbuf.at[0, 0:3]),
+        ("bx", wbuf.at[0:3, 0:7, 0]), ("az", wbuf.at[0:3, 0:4, 0]), ("afar", wbuf.at[0:3, 0:3, 0]),
         ("pos", pos_sib), ("emb", emb_sib), ("mark x", marks_mid.at[0:3]), ("mark z", marks_got.at[0:7]),
         ("out x", xout), ("out z", got.at[0:7]), ("half", seqh.at[0]), ("fin", fin.at[0]),
         ("pair 0", c2.at[0:5]), ("pair 1", c2.at[0:3]),

time: 76.6 us -> 74.4 us (0.971)
  Pallas kernels: 74.9 us -> 72.7 us
    pallas_call x1, Pallas kernels: 74.9 us -> 72.7 us  [local(): pl.pallas_call(kernel, out_shape=jax.ShapeDtypeStruct((TOK_DEV, HALF), BF...]
where the time goes in v5:
time: 74.4 us; the launch traced here: 74.2 us
  Pallas kernels  72.7 us (98%)
  local copies, waits for them, and re-layouts  1.54 us (2%)
    pallas_call x1, Pallas kernels, local(): pl.pallas_call(kernel, out_shape=jax.ShapeDtypeStruct((TOK_DEV, HALF), BF...  72.7 us
    unnamed x1, local copies, waits for them, and re-layouts  1.54 us

profile of v5, /device:TPU:1, one launch (start us, length us, event | category | flops | bytes accessed | tf_op | source)
XLA Modules:
  0.0 74.2 jit_solution(1408228159047216938)
XLA Ops:
  0.0 72.7 %shard_map.46 = bf16[128,384]{1,0:T(8,128)(2,1)} custom-call(bf16[256,1536]{1,0:T(8,128)(2,1)} %emb_in.1, s32[1,256]{1,0:T(1,128)} %bitcast.1, bf16[24,768]{1,0:T(8,128)(2,1)} %w_in.1, bf16[768,1152]{1,0:T(8,128)(2,1)} %aw_in.1), custom_call_target="tpu_custom_call" | custom-call | tf_op jit(solution)/shard_map/pallas_call | solution.py:535
  72.7 1.5 %copy.6 = bf16[128,384]{1,0:T(8,128)(2,1)} copy(bf16[128,384]{1,0:T(8,128)(2,1)} %shard_map.46) | data formatting | bytes 196608

commit v6 on v5

--- a/solution.py
+++ b/solution.py
@@ -96,7 +96,7 @@
         load.start()
 
     barrier = pltpu.get_barrier_semaphore()
-    partners = [sibling] + [dev(x_of[d], z, c) for d in (1, 2, 3)] + [dev(x, z_of[d], c) for d in range(1, 8)]
+    partners = [sibling] + [dev(x_of[d], z, c) for d in (1, 2, 3)] + [dev(x, z_of[d], c) for d in (1, 2, 6, 7)]
     partners += [dev(x_of[d], z, 1 - c) for d in (1, 2, 3)] + [dev(x, z_of[d], 1 - c) for d in (1, 2, 6, 7)]
     for partner in partners:
         pl.semaphore_signal(barrier, inc=1, device_id=partner, device_id_type=MESH)
@@ -410,23 +410,26 @@
         for _ in range(min(count, len(tasks))):
             tasks.pop(0)()
 
-    def arrived_head(way, s, h):
+    def heads(head, *args):
+        for h in range(3):
+            head(*args, h)
+
+    def arrived(way, s):
         zo = origin(way, s + 1)
         if s == 3:
-            pl.when(low_got(in_seg[way], s))(lambda: part_head(zo, h))
+            pl.when(low_got(in_seg[way], s))(lambda: heads(part_head, zo))
         else:
             full = rest_got(in_seg[way], s)
-            pl.when(full)(lambda: full_head(zo, h))
-            pl.when(jnp.logical_not(full))(lambda: part_head(zo, h))
+            pl.when(full)(lambda: heads(full_head, zo))
+            pl.when(jnp.logical_not(full))(lambda: heads(part_head, zo))
 
     def later(action, *args):
         tasks.append(lambda: action(*args))
 
-    for h in range(3):
-        full_head(z, h, fresh=True)
+    later(lambda: [full_head(z, h, fresh=True) for h in range(3)])
     for s in range(4):
         for k in (0, 1):
-            run(1)
+            run(1 if s else k)
             for way in (0, 1):
                 take_piece(way, "low", s, k)
                 if s < 3:
@@ -437,23 +440,19 @@
                 )
         if s < 3:
             for k in (0, 1):
-                run(2)
+                run(1 - k)
                 for way in (0, 1):
                     take_piece(way, "rest", s, k)
                     if s < 2:
                         pass_on(way, "rest", s + 1, k)
         for way in (0, 1):
-            for h in range(3):
-                later(arrived_head, way, s, h)
+            later(arrived, way, s)
         if s == 2:
-            run(3)
             take(c2.at[0:5], "pair 0")
-            for h in range(3):
-                later(pair_head, (0, 7, 1, 6, 2), h)
+            later(heads, pair_head, (0, 7, 1, 6, 2))
     run(len(tasks))
     take(c2.at[0:3], "pair 1")
-    for h in range(3):
-        pair_head((3, 5, 4), h)
+    heads(pair_head, (3, 5, 4))
 
     heads = [acc_s[h] / l_s[h] for h in range(3)]
     done = jnp.concatenate(

time: 74.4 us -> 73.2 us (0.984)
  Pallas kernels: 72.7 us -> 71.6 us
    pallas_call x1, Pallas kernels: 72.7 us -> 71.6 us  [local(): pl.pallas_call(kernel, out_shape=jax.ShapeDtypeStruct((TOK_DEV, HALF), BF...]
where the time goes in v6:
time: 73.2 us; the launch traced here: 73.1 us
  Pallas kernels  71.6 us (98%)
  local copies, waits for them, and re-layouts  1.54 us (2%)
    pallas_call x1, Pallas kernels, local(): pl.pallas_call(kernel, out_shape=jax.ShapeDtypeStruct((TOK_DEV, HALF), BF...  71.6 us
    unnamed x1, local copies, waits for them, and re-layouts  1.54 us

profile of v6, /device:TPU:1, one launch (start us, length us, event | category | flops | bytes accessed | tf_op | source)
XLA Modules:
  0.0 73.1 jit_solution(17421300207268187280)
XLA Ops:
  0.0 71.6 %shard_map.46 = bf16[128,384]{1,0:T(8,128)(2,1)} custom-call(bf16[256,1536]{1,0:T(8,128)(2,1)} %emb_in.1, s32[1,256]{1,0:T(1,128)} %bitcast.1, bf16[24,768]{1,0:T(8,128)(2,1)} %w_in.1, bf16[768,1152]{1,0:T(8,128)(2,1)} %aw_in.1), custom_call_target="tpu_custom_call" | custom-call | tf_op jit(solution)/shard_map/pallas_call | solution.py:534
  71.6 1.5 %copy.6 = bf16[128,384]{1,0:T(8,128)(2,1)} copy(bf16[128,384]{1,0:T(8,128)(2,1)} %shard_map.46) | data formatting | bytes 196608

commit v7 on v6

--- a/solution.py
+++ b/solution.py
@@ -41,7 +41,7 @@
     pos_ref, w_ref,
     emb_own, emb_sib, pos_sib, wbuf, awbuf, awc,
     marks, marks_mid, marks_z, marks_got,
-    hot_s, seq, mid, got, xout, kv, c2, qm, m_s, l_s, acc_s, mask_s, low_mask_s, fin, seqh,
+    hot_s, seq, mid, got, xout, kv, c2, qm, m_s, l_s, acc_s, mask_s, low_mask_s, place_s, back_s, fin, seqh,
     sems, local_sems,
 ):
     me = lax.axis_index("seq")
@@ -265,10 +265,9 @@
     group = row // 32
     first_wanted = row % 32 * 4 + group % 2 * 2 + group // 2 + 1
 
-    def place(oc, zo_marks, rows):
+    def place(oc, zo_marks):
         wanted = (first_wanted + oc * 128).astype(F32)
-        hot = (zo_marks[:, oc * 64 : oc * 64 + 64] == wanted).astype(F32).astype(BF16)
-        return jnp.dot(hot, rows.reshape(64, HALF), preferred_element_type=F32)
+        return (zo_marks[:, oc * 64 : oc * 64 + 64] == wanted).astype(F32)
 
     def project(h, oc):
         w = awc[pl.ds(pl.multiple_of(h * HALF, 128), HALF), :]
@@ -279,13 +278,23 @@
         return jnp.dot(rows, w, preferred_element_type=F32)
 
     take(marks_got.at[0:7], "mark z")
+    all_marks = [marks_z[z][0:1]] + [marks_got[(z - d) % NZ][0:1] for d in (1, 7, 2, 6, 3, 5, 4)]
+    for oc in (0, 1):
+        place_s[oc] = jnp.concatenate([place(oc, marked) for marked in all_marks], axis=1).astype(BF16)
+
+    p_row, n_col = iota((128, 256), 0), iota((128, 256), 1)
+    for n, oc in enumerate((1 - c, c)):
+        res = p_row % 4
+        source = jnp.where(res % 2 == c, 0, 128) + (res // 2) * 64 + oc * 32 + p_row // 4
+        back_s[n] = (n_col == source).astype(F32).astype(BF16)
 
     def projections_of(oc):
-        total = place(oc, marks_z[z][0:1], mid[:, z, oc])
+        blocks = [mid[:, z, oc].reshape(64, HALF)]
         for d in (1, 7, 2, 6, 3, 5, 4):
             zo = (z - d) % NZ
             take(got.at[zo, oc], ("out z", d, oc))
-            total = total + place(oc, marks_got[zo][0:1], got[zo, oc])
+            blocks.append(got[zo, oc].reshape(64, HALF))
+        total = jnp.dot(place_s[oc], jnp.concatenate(blocks, axis=0), preferred_element_type=F32)
         seqh[c, oc] = total.astype(BF16)
         put(seqh.at[c, oc], seqh.at[c, oc], sibling, "half", ("half", oc))
         part = project(c, oc)
@@ -458,13 +467,8 @@
     done = jnp.concatenate(
         [jnp.where(lane256 < 64, heads[0], heads[1]), heads[2]], axis=1
     ).astype(BF16)
-    p_row, n_col = iota((128, 256), 0), iota((128, 256), 1)
-
-    def arranged(oc):
-        res = p_row % 4
-        source = jnp.where(res % 2 == c, 0, 128) + (res // 2) * 64 + oc * 32 + p_row // 4
-        hot = (n_col == source).astype(F32).astype(BF16)
-        rows = jnp.dot(hot, done, preferred_element_type=F32)
+    def arranged(n):
+        rows = jnp.dot(back_s[n], done, preferred_element_type=F32)
         a, b = rows[:, 0:128], rows[:, 128:256]
         a_rolled, b_rolled = roll64(a), roll64(b)
         return jnp.concatenate([
@@ -473,9 +477,9 @@
             jnp.where(c == 0, a_rolled, a),
         ], axis=1)
 
-    fin[0] = arranged(1 - c).astype(BF16)
+    fin[0] = arranged(0).astype(BF16)
     put(fin.at[0], fin.at[1], sibling, "fin", "fin")
-    mine = arranged(c)
+    mine = arranged(1)
     take(fin.at[1], "fin")
     own_lane = (iota((128, HALF), 1) // 64) % 2 == c
     out_ref[...] = jnp.where(own_lane, mine, fin[1].astype(F32)).astype(BF16)
@@ -526,6 +530,8 @@
         pltpu.VMEM((3, 256, 128), F32),
         pltpu.VMEM((2, 128, 256), F32),
         pltpu.VMEM((2, 128, 128), F32),
+        pltpu.VMEM((2, 128, 512), BF16),
+        pltpu.VMEM((2, 128, 256), BF16),
         pltpu.VMEM((2, 128, HALF), BF16),
         pltpu.VMEM((2, 2, 128, HALF), BF16),
         pltpu.SemaphoreType.DMA((N_SEMS,)),

time: 73.2 us -> 73.1 us (level)
  no operation moved by 1% of the time
where the time goes in v7:
time: 73.1 us; the launch traced here: 73 us
  Pallas kernels  71.4 us (98%)
  local copies, waits for them, and re-layouts  1.54 us (2%)
    pallas_call x1, Pallas kernels, local(): pl.pallas_call(kernel, out_shape=jax.ShapeDtypeStruct((TOK_DEV, HALF), BF...  71.4 us
    unnamed x1, local copies, waits for them, and re-layouts  1.54 us

profile of v7, /device:TPU:1, one launch (start us, length us, event | category | flops | bytes accessed | tf_op | source)
XLA Modules:
  0.0 73.0 jit_solution(67036001729759034)
XLA Ops:
  0.0 71.4 %shard_map.46 = bf16[128,384]{1,0:T(8,128)(2,1)} custom-call(bf16[256,1536]{1,0:T(8,128)(2,1)} %emb_in.1, s32[1,256]{1,0:T(1,128)} %bitcast.1, bf16[24,768]{1,0:T(8,128)(2,1)} %w_in.1, bf16[768,1152]{1,0:T(8,128)(2,1)} %aw_in.1), custom_call_target="tpu_custom_call" | custom-call | tf_op jit(solution)/shard_map/pallas_call | solution.py:540
  71.4 1.5 %copy.6 = bf16[128,384]{1,0:T(8,128)(2,1)} copy(bf16[128,384]{1,0:T(8,128)(2,1)} %shard_map.46) | data formatting | bytes 196608
